TPU v7x, 32 devices: a whole 2x2x4 slice. The times are simulated.
32 devices in a mesh: ten: 16 (over z, x, core), fsdp: 2 (over y).
Axes of the slice: x: 2, y: 2, z: 4, core: 2. Of those that a mesh axis runs over, the one named last changes fastest.
Arguments:
- activations: bfloat16 [16, 32, 32, 1280], P('ten', 'fsdp'), may hold values from -6 to 6
- cotangent: bfloat16 [16, 32, 32, 1280], P('ten', 'fsdp'), may hold values from -6 to 6
- base_kernel: bfloat16 [3, 1280, 3, 1280], P(None, 'fsdp'), may hold values from -0.0546875 to 0.0546875
- down_table: bfloat16 [16, 3, 3, 32, 1280], P(None, None, None, 'fsdp', 'ten'), may hold values from -0.0546875 to 0.0546875
- up_table: bfloat16 [16, 32, 1280], P(None, None, 'ten'), may hold values from -1 to 1
- sample_tenant: int32 [16], P('ten'), may hold values from 0 to 15
- tenant_slot: int32 [16], replicated, may hold values from 0 to 15, each once
- timesteps: int32 [16], P('ten'), may hold values from 0 to 999
Outputs:
- block_out: bfloat16 [16, 32, 32, 1280], P('ten', 'fsdp')
- down_grad: bfloat16 [16, 3, 3, 32, 1280], P(None, None, None, 'fsdp', 'ten')
- up_grad: bfloat16 [16, 32, 1280], P(None, None, 'ten')
All inputs are finite; a program needn't handle non-finite values.
Results may differ from a plain program's by a relative error of at most 0.0066.
Values may be sent and summed in bfloat16 or wider, within the bound.
A program may use at most 128 MiB of HBM per device.

v0:
```python
import jax
import jax.numpy as jnp
from jax import lax
from jax.sharding import PartitionSpec as P


def conv_same(field, kernel):
    return lax.conv_general_dilated(
        field,
        kernel,
        (1, 1),
        "SAME",
        dimension_numbers=("NHWC", "HWIO", "NHWC"),
        preferred_element_type=jnp.float32,
    )


def slope_of(block, cotangent, weight):
    value = block.astype(jnp.float32)
    sigma = jax.nn.sigmoid(value)
    return (cotangent.astype(jnp.float32) * weight * sigma * (1.0 + value * (1.0 - sigma))).astype(
        jnp.bfloat16
    )


def local(
    activations, cotangent, base_kernel, down_table, up_table, sample_tenant, tenant_slot, timesteps
):
    width = base_kernel.shape[1]
    kernel_hwio = jnp.transpose(base_kernel, (0, 2, 3, 1))
    ten_index = lax.axis_index("ten")
    fsdp_index = lax.axis_index("fsdp")
    tenants = down_table.shape[0]
    rank = up_table.shape[1]
    block_cols = down_table.shape[4]
    all_tenants = lax.all_gather(sample_tenant, "ten", axis=0, tiled=True)
    all_slots = tenant_slot[all_tenants]
    groups = all_slots.shape[0]
    picks = (all_slots[:, None] == jnp.arange(tenants, dtype=jnp.int32)[None, :]).astype(
        jnp.bfloat16
    )
    send_down = jnp.einsum(
        "dl,labkc->dabkc", picks, down_table, preferred_element_type=jnp.float32
    ).astype(jnp.bfloat16)
    send_up = jnp.einsum("dl,lkc->dkc", picks, up_table, preferred_element_type=jnp.float32).astype(
        jnp.bfloat16
    )
    send_up = send_up.reshape(groups, 1, 1, rank, block_cols)
    recv_down, recv_up = (
        lax.all_to_all(send_down, "ten", split_axis=0, concat_axis=4, tiled=True),
        lax.all_to_all(send_up, "ten", split_axis=0, concat_axis=4, tiled=True),
    )
    down_fac = recv_down[0]
    up_whole = recv_up[0, 0, 0]
    up_fac = lax.dynamic_slice_in_dim(up_whole, fsdp_index * width, width, 1)
    whole = lax.all_gather(activations, "fsdp", axis=1, tiled=True)
    height = whole.shape[1]
    breadth = whole.shape[2]
    cells = height * breadth
    base_part = conv_same(whole, kernel_hwio).astype(jnp.bfloat16)
    low_slice = conv_same(whole, jnp.transpose(down_fac, (0, 1, 3, 2))).astype(jnp.bfloat16)
    low = lax.all_gather(low_slice, "fsdp", axis=3, tiled=True).reshape(cells, rank)
    y_cols = (
        base_part.reshape(cells, width).astype(jnp.float32)
        + jnp.dot(low, up_fac, preferred_element_type=jnp.float32)
    ).astype(jnp.bfloat16)
    y_cols = y_cols.reshape(1, height, breadth, width)
    block_out = lax.all_to_all(y_cols, "fsdp", split_axis=1, concat_axis=3, tiled=True)
    weight = 1.0 / (1.0 + timesteps[0].astype(jnp.float32) / 250.0)
    slope = lax.all_to_all(
        slope_of(block_out, cotangent, weight), "fsdp", split_axis=3, concat_axis=1, tiled=True
    )
    slope = slope.reshape(cells, width)
    up_term = lax.dot_general(
        low, slope, (((0,), (0,)), ((), ())), preferred_element_type=jnp.float32
    ).astype(jnp.bfloat16)
    grad_part = lax.dot_general(
        slope, up_fac, (((1,), (1,)), ((), ())), preferred_element_type=jnp.float32
    )
    low_grad = lax.psum_scatter(grad_part, "fsdp", scatter_dimension=1, tiled=True).astype(
        jnp.bfloat16
    )
    padded = jnp.pad(whole[0], ((1, 1), (1, 1), (0, 0)))
    channels = whole.shape[3]
    rows_list = []
    for tap_row in range(3):
        cols_list = []
        for tap_col in range(3):
            shifted = padded[tap_row : tap_row + height, tap_col : tap_col + breadth].reshape(
                cells, channels
            )
            cols_list.append(
                lax.dot_general(
                    low_grad, shifted, (((0,), (0,)), ((), ())), preferred_element_type=jnp.float32
                )
            )
        rows_list.append(jnp.stack(cols_list))
    down_term = jnp.stack(rows_list).astype(jnp.bfloat16)
    up_all = lax.all_gather(up_term, "fsdp", axis=1, tiled=True)
    start_buffers = (
        jnp.zeros((groups,) + down_term.shape[:3] + (block_cols,), jnp.bfloat16),
        jnp.zeros((groups, 1, 1, rank, block_cols), jnp.bfloat16),
    )
    down_piece = lax.dynamic_slice_in_dim(
        lax.all_gather(down_term[None], "ten", axis=0, tiled=True),
        ten_index * block_cols,
        block_cols,
        4,
    )
    up_piece = lax.dynamic_slice_in_dim(
        lax.all_gather(up_all[None, None, None], "ten", axis=0, tiled=True),
        ten_index * block_cols,
        block_cols,
        4,
    )
    up_new = lax.dynamic_update_slice_in_dim(start_buffers[1], up_piece, jnp.int32(0), 0)
    down_sum = jnp.einsum("dl,dabkc->labkc", picks, down_piece, preferred_element_type=jnp.float32)
    up_sum = jnp.einsum("dl,dkc->lkc", picks, up_new[:, 0, 0], preferred_element_type=jnp.float32)
    return (block_out, down_sum.astype(jnp.bfloat16), up_sum.astype(jnp.bfloat16))


def solution(mesh):
    placed = (
        P("ten", "fsdp", None, None),
        P("ten", "fsdp", None, None),
        P(None, "fsdp", None, None),
        P(None, None, None, "fsdp", "ten"),
        P(None, None, "ten"),
        P("ten"),
        P(),
        P("ten"),
    )
    return jax.shard_map(
        local,
        mesh=mesh,
        in_specs=placed,
        out_specs=(
            P("ten", "fsdp", None, None),
            P(None, None, None, "fsdp", "ten"),
            P(None, None, "ten"),
        ),
        check_vma=False,
    )
```

profile of v0, /device:TPU:11, one launch (start us, length us, event | category | flops | bytes accessed | tf_op | source)
XLA Modules:
  0.0 330.8 jit_solution(12981015446324946231)
XLA Ops:
  7.3 3.2 copy.129
  11.1 0.6 dynamic-slice
  11.7 0.8 dynamic-update-slice
  12.5 7.9 %all-reduce.1 = s32[16]{0:T(128)S(1)} all-reduce(s32[16]{0:T(128)S(1)} %dynamic-update-slice), channel_id=1, replica_groups=mesh['ten'=16,'fsdp'=2] {'ten'}, use_global_device_ids=true, to_apply=%add.1 | all-reduce | flops 16 | bytes 128
  20.3 0.7 gather_fusion
  21.3 0.7 copy.142
  21.9 8.5 %all-to-all-start.1 = ((bf16[16,1,1,32,80]{4,3,2,1,0:T(8,128)(2,1)}), bf16[16,1,1,32,80]{4,3,2,1,0:T(8,128)(2,1)S(1)}, u32[]{:S(2)}, u32[]{:S(2)}) async-start(bf16[16,1,1,32,80]{4,3,2,1,0:T(8,128)(2,1)} %copy.142), calls=%async_computation.1 | async-start | bytes 262144 | tf_op jit(solution)/shard_map/all_to_all | solution.py:51
  30.8 1.0 copy.136
  31.8 3.9 %all-to-all-done.1 = bf16[16,1,1,32,80]{4,3,2,1,0:T(8,128)(2,1)S(1)} async-done(((bf16[16,1,1,32,80]{4,3,2,1,0:T(8,128)(2,1)}), bf16[16,1,1,32,80]{4,3,2,1,0:T(8,128)(2,1)S(1)}, u32[]{:S(2)}, u32[]{:S(2)}) %all-to-all-start.1) | async-done | bytes 81952 | tf_op jit(solution)/shard_map/all_to_all | solution.py:51
  35.6 6.7 %all-to-all-start = ((bf16[16,3,3,16,80]{4,3,2,1,0:T(8,128)(2,1)}), bf16[16,3,3,16,80]{4,3,2,1,0:T(8,128)(2,1)S(1)}, u32[]{:S(2)}, u32[]{:S(2)}) async-start(bf16[16,3,3,16,80]{4,3,2,1,0:T(8,128)(2,1)} %copy.136), calls=%async_computation | async-start | bytes 1179648 | tf_op jit(solution)/shard_map/all_to_all | solution.py:50
  42.5 14.7 %all-to-all-done = bf16[16,3,3,16,80]{4,3,2,1,0:T(8,128)(2,1)S(1)} async-done(((bf16[16,3,3,16,80]{4,3,2,1,0:T(8,128)(2,1)}), bf16[16,3,3,16,80]{4,3,2,1,0:T(8,128)(2,1)S(1)}, u32[]{:S(2)}, u32[]{:S(2)}) %all-to-all-start) | async-done | bytes 368672 | tf_op jit(solution)/shard_map/all_to_all | solution.py:50
  57.4 0.6 squeeze.13
  58.0 2.1 pad.5
  60.1 1.8 copy.131
  62.2 1.4 copy-done.18
  63.6 7.8 %fusion.19 = bf16[32,8,5,16]{3,1,2,0:T(8,128)(2,1)S(1)} fusion(bf16[3,3,16,1280]{3,2,1,0:T(8,128)(2,1)S(1)} %squeeze.13, bf16[32,1,7,2,1280]{4,2,3,0,1:T(8,128)(2,1)S(1)} %slice.39, bf16[32,1,8,5,1280]{4,2,3,0,1:T(8,128)(2,1)S(1)} %copy.131), kind=kOutput, calls=%fused_computation.42 | convolution fusion | flops 475791360 | bytes 4833280 | tf_op jit(solution)/shard_map/conv_general_dilated | solution.py:8
  71.8 28.3 %select_convert_fusion = bf16[32,8,5,640]{3,1,2,0:T(8,128)(2,1)S(1)} fusion(bf16[3,640,3,1280]{3,1,2,0:T(8,128)(2,1)} %param.10, bf16[32,1,7,2,1280]{4,2,3,0,1:T(8,128)(2,1)S(1)} %slice.39, bf16[32,1,8,5,1280]{4,2,3,0,1:T(8,128)(2,1)} %copy-done.18, pred[8,5]{0,1:T(8,128)(4,1)S(1)} %copy-done.23), kind=kOutput, calls=%fused_computation.13 | convolution fusion | flops 18496552960 | bytes 20807720 | tf_op jit(solution)/shard_map/conv_general_dilated | solution.py:8
  100.3 5.6 %all-gather = bf16[32,1,32,32]{0,3,2,1:T(8,128)(2,1)S(1)} all-gather(bf16[32,1,32,16]{0,3,2,1:T(8,128)(2,1)S(1)} %slice.41), channel_id=2, replica_groups=mesh['ten'=16,'fsdp'=2] {'fsdp'}, dimensions={3}, use_global_device_ids=true | all-gather | bytes 98304 | tf_op jit(solution)/shard_map/all_gather | solution.py:62
  106.8 1.5 copy.133
  108.3 1.6 fusion.9
  109.9 3.8 %all-to-all-start.2 = ((bf16[1,32,32,640]{3,2,0,1:T(8,128)(2,1)}), bf16[1,32,32,640]{3,2,0,1:T(8,128)(2,1)S(1)}, u32[]{:S(2)}, u32[]{:S(2)}) async-start(bf16[1,32,32,640]{3,2,0,1:T(8,128)(2,1)} %bitcast.15), calls=%async_computation.2 | async-start | bytes 2621440 | tf_op jit(solution)/shard_map/all_to_all | solution.py:68
  114.4 14.7 %all-to-all-done.2 = bf16[1,32,32,640]{3,2,0,1:T(8,128)(2,1)S(1)} async-done(((bf16[1,32,32,640]{3,2,0,1:T(8,128)(2,1)}), bf16[1,32,32,640]{3,2,0,1:T(8,128)(2,1)S(1)}, u32[]{:S(2)}, u32[]{:S(2)}) %all-to-all-start.2) | async-done | bytes 1310752 | tf_op jit(solution)/shard_map/all_to_all | solution.py:68
  129.1 1.3 copy.180
  130.5 0.9 all_to_all.55
  131.4 2.9 fusion.8
  134.3 5.7 %copy.146 = bf16[1,16,32,1280]{2,1,0,3:T(8,128)(2,1)} copy(bf16[1,16,32,1280]{3,2,1,0:T(8,128)(2,1)S(1)} %fusion.8) | data formatting | bytes 2621440 | tf_op jit(solution)/shard_map/convert_element_type | solution.py:21
  140.0 7.7 %reshape.213 = bf16[2,2,163840]{2,1,0:T(2,128)(2,1)} reshape(bf16[1280,1,16,32]{3,2,1,0:T(8,128)(2,1)} %bitcast.118) | data formatting | bytes 2621440
  147.7 4.8 %all-to-all-start.3 = ((bf16[2,2,163840]{2,1,0:T(2,128)(2,1)}), bf16[2,2,163840]{2,1,0:T(2,128)(2,1)}, u32[]{:S(2)}, u32[]{:S(2)}) async-start(bf16[2,2,163840]{2,1,0:T(2,128)(2,1)} %reshape.213), calls=%async_computation.3 | async-start | bytes 2621440 | tf_op jit(solution)/shard_map/all_to_all | solution.py:70
  152.6 11.0 %pad_slice_fusion.7 = (bf16[32,32,1280]{2,0,1:T(8,128)(2,1)}, bf16[32,32,1280]{2,0,1:T(8,128)(2,1)}, bf16[32,32,1280]{2,0,1:T(8,128)(2,1)}, bf16[32,32,1280]{2,0...) fusion(bf16[32,32,1280]{2,0,1:T(8,128)(2,1)S(1)} %bitcast.117), kind=kLoop, calls=%fused_computation.12 | loop fusion | bytes 23592960 | tf_op jit(solution)/shard_map/slice | solution.py:89
  163.6 4.8 %copy.149 = bf16[32,32,1280]{2,1,0:T(8,128)(2,1)} copy(bf16[32,32,1280]{2,0,1:T(8,128)(2,1)} %get-tuple-element.21) | data formatting | bytes 5242880 | tf_op jit(solution)/shard_map/slice | solution.py:89
  168.4 3.0 copy.150
  171.4 3.0 copy.151
  174.5 2.9 copy.152
  177.4 2.9 copy.154
  180.4 2.9 copy.155
  183.3 3.0 copy.156
  186.3 3.2 copy.157
  189.5 2.9 copy.153
  192.4 5.3 %reshape.214 = bf16[1280,1,16,32]{3,2,1,0:T(8,128)(2,1)} reshape(bf16[2,2,163840]{2,1,0:T(2,128)(2,1)} %all-to-all-done.3) | data formatting | bytes 2621440
  197.7 8.1 %copy.167 = bf16[1,16,32,2,640]{4,3,2,1,0:T(2,128)(2,1)S(1)} copy(bf16[1,16,32,2,640]{2,1,4,3,0:T(8,128)(2,1)} %bitcast.119) | data formatting | bytes 2621440 | tf_op jit(solution)/shard_map/all_to_all | solution.py:70
  206.0 1.2 fusion.28
  207.6 3.8 %all_gather.22 = bf16[32,1280]{1,0:T(8,128)(2,1)} all-gather(bf16[32,640]{1,0:T(8,128)(2,1)S(1)} %convolution_convert_fusion.13), channel_id=1, replica_groups=mesh['ten'=16,'fsdp'=2] {'fsdp'}, dimensions={1}, use_global_device_ids=true | all-gather | bytes 122880 | tf_op jit(solution)/shard_map/all_gather | solution.py:99
  211.4 7.8 %reduce-scatter.2.cloned.1.call-done = f32[1024,16]{0,1:T(8,128)} async-done(((f32[1024,32]{0,1:T(8,128)}), f32[1024,16]{0,1:T(8,128)}) %reduce-scatter.2.cloned.1.call-update) | async-done | bytes 65552 | tf_op jit(solution)/shard_map/reduce_scatter | solution.py:80
  219.2 0.8 convert_element_type.80
  220.1 2.3 fusion.16
  222.4 0.5 fusion.17
  222.9 0.5 fusion.18
  223.3 0.8 copy-done.9
  224.2 0.4 fusion.14
  224.6 0.4 copy-done.4
  225.0 0.4 fusion.10
  225.5 0.6 copy-done.5
  226.1 0.4 fusion.11
  226.9 0.4 fusion.12
  227.4 0.7 copy-done.7
  228.1 0.4 fusion.13
  228.8 0.4 fusion.15
  229.3 0.8 pad_maximum_fusion
  230.1 29.0 %all-gather.10.cloned.1.call-done = bf16[512,1280]{1,0:T(8,128)(2,1)} async-done(((bf16[32,1280]{1,0:T(8,128)(2,1)}), bf16[512,1280]{1,0:T(8,128)(2,1)}) %all-gather.10.cloned.1.call-update) | async-done | bytes 1310736 | tf_op jit(solution)/shard_map/all_gather | solution.py:111
  259.1 1.1 constant_dynamic-slice_fusion
  260.4 0.7 copy.161
  261.1 60.2 %all-gather.8.cloned.1.call-done = bf16[16,3,3,16,1280]{4,3,2,1,0:T(8,128)(2,1)} async-done(((bf16[1,3,3,16,1280]{4,3,2,1,0:T(8,128)(2,1)}), bf16[16,3,3,16,1280]{4,3,2,1,0:T(8,128)(2,1)}) %all-gather.8.cloned.1.call-update) | async-done | bytes 5898256 | tf_op jit(solution)/shard_map/all_gather | solution.py:105
  321.3 1.5 constant_dynamic-slice_fusion.1
  323.1 1.0 copy.160
  (75 shorter events, 4.9 us)
Async XLA Ops:
  7.2 23.2 %copy-start = (bf16[16,3,3,16,80]{4,3,2,1,0:T(8,128)(2,1)S(1)}, bf16[16,3,3,16,80]{4,3,2,1,0:T(8,128)(2,1)}, u32[]{:S(2)}) copy-start(bf16[16,3,3,16,80]{4,3,2,1,0:T(8,128)(2,1)} %param.11) | copy-start | bytes 1105924
  7.2 3.9 %copy-start.22 = (u32[32]{0:T(128)S(1)}, u32[32]{0:T(128)}, u32[]{:S(2)}) copy-start(u32[32]{0:T(128)} %constant.49) | copy-start | bytes 388
  7.2 13.2 %copy-start.2 = (s32[16]{0:T(128)S(1)}, s32[16]{0:T(128)}, u32[]{:S(2)}) copy-start(s32[16]{0:T(128)} %param.14) | copy-start | bytes 196
  7.2 13.8 %copy-start.20 = (bf16[16,32,80]{2,1,0:T(8,128)(2,1)S(1)}, bf16[16,32,80]{2,1,0:T(8,128)(2,1)}, u32[]{:S(2)}) copy-start(bf16[16,32,80]{2,1,0:T(8,128)(2,1)} %param.12) | copy-start | bytes 245764
  7.2 50.7 %all-gather.6.cloned.1.call-start = ((), (), s32[]{:S(2)}) async-start(), calls=%async_computation.5 | async-start | bytes 3932160 | tf_op jit(solution)/shard_map/all_gather | solution.py:56
  21.9 13.7 %all-to-all-start.1 = ((bf16[16,1,1,32,80]{4,3,2,1,0:T(8,128)(2,1)}), bf16[16,1,1,32,80]{4,3,2,1,0:T(8,128)(2,1)S(1)}, u32[]{:S(2)}, u32[]{:S(2)}) async-start(bf16[16,1,1,32,80]{4,3,2,1,0:T(8,128)(2,1)} %copy.142), calls=%async_computation.1 | async-start | bytes 262144 | tf_op jit(solution)/shard_map/all_to_all | solution.py:51
  35.6 21.6 %all-to-all-start = ((bf16[16,3,3,16,80]{4,3,2,1,0:T(8,128)(2,1)}), bf16[16,3,3,16,80]{4,3,2,1,0:T(8,128)(2,1)S(1)}, u32[]{:S(2)}, u32[]{:S(2)}) async-start(bf16[16,3,3,16,80]{4,3,2,1,0:T(8,128)(2,1)} %copy.136), calls=%async_computation | async-start | bytes 1179648 | tf_op jit(solution)/shard_map/all_to_all | solution.py:50
  61.9 1.7 copy-start.18
  63.5 8.1 %copy-start.21 = (pred[8,5]{1,0:T(8,128)(4,1)S(1)}, pred[8,5]{1,0:T(8,128)(4,1)}, u32[]{:S(2)}) copy-start(pred[8,5]{1,0:T(8,128)(4,1)} %constant.45) | copy-start | bytes 124
  63.5 8.2 %copy-start.23 = (pred[8,5]{0,1:T(8,128)(4,1)S(1)}, pred[8,5]{0,1:T(8,128)(4,1)}, u32[]{:S(2)}) copy-start(pred[8,5]{0,1:T(8,128)(4,1)} %constant.53) | copy-start | bytes 124
  109.9 19.2 %all-to-all-start.2 = ((bf16[1,32,32,640]{3,2,0,1:T(8,128)(2,1)}), bf16[1,32,32,640]{3,2,0,1:T(8,128)(2,1)S(1)}, u32[]{:S(2)}, u32[]{:S(2)}) async-start(bf16[1,32,32,640]{3,2,0,1:T(8,128)(2,1)} %bitcast.15), calls=%async_computation.2 | async-start | bytes 2621440 | tf_op jit(solution)/shard_map/all_to_all | solution.py:68
  131.4 8.6 %copy-start.19 = (bf16[1,16,32,1280]{3,2,1,0:T(8,128)(2,1)}, bf16[1,16,32,1280]{3,2,1,0:T(8,128)(2,1)S(1)}, u32[]{:S(2)}) copy-start(bf16[1,16,32,1280]{3,2,1,0:T(8,128)(2,1)S(1)} %all_to_all.55) | copy-start | bytes 3932164
  147.7 4.9 %copy-start.3 = (bf16[1,32,32,1280]{3,1,2,0:T(8,128)(2,1)S(1)}, bf16[1,32,32,1280]{3,1,2,0:T(8,128)(2,1)}, u32[]{:S(2)}) copy-start(bf16[1,32,32,1280]{3,1,2,0:T(8,128)(2,1)} %all-gather.6.cloned.1.call-done) | copy-start | bytes 7864324
  147.7 44.7 %all-to-all-start.3 = ((bf16[2,2,163840]{2,1,0:T(2,128)(2,1)}), bf16[2,2,163840]{2,1,0:T(2,128)(2,1)}, u32[]{:S(2)}, u32[]{:S(2)}) async-start(bf16[2,2,163840]{2,1,0:T(2,128)(2,1)} %reshape.213), calls=%async_computation.3 | async-start | bytes 2621440 | tf_op jit(solution)/shard_map/all_to_all | solution.py:70
  152.5 66.7 %reduce-scatter.2.cloned.1.call-start = ((), (), s32[]{:S(2)}) async-start(), calls=%async_computation.6 | async-start | bytes 196608 | tf_op jit(solution)/shard_map/reduce_scatter | solution.py:80
  163.6 4.9 %copy-start.17 = (bf16[32,32,1280]{2,0,1:T(8,128)(2,1)S(1)}, bf16[32,32,1280]{2,0,1:T(8,128)(2,1)}, u32[]{:S(2)}) copy-start(bf16[32,32,1280]{2,0,1:T(8,128)(2,1)} %get-tuple-element.22) | copy-start | bytes 7864324
  168.4 3.0 copy-start.16
  171.4 3.0 copy-start.15
  174.5 2.9 copy-start.14
  177.4 3.0 copy-start.13
  180.4 2.9 copy-start.12
  207.2 51.9 %all-gather.10.cloned.1.call-start = ((), (), s32[]{:S(2)}) async-start(), calls=%async_computation.8 | async-start | bytes 1392640 | tf_op jit(solution)/shard_map/all_gather | solution.py:111
  207.6 14.8 %copy-start.10 = (bf16[32,32,1280]{2,1,0:T(8,128)(2,1)S(1)}, bf16[32,32,1280]{2,1,0:T(8,128)(2,1)}, u32[]{:S(2)}) copy-start(bf16[32,32,1280]{2,1,0:T(8,128)(2,1)} %copy.156) | copy-start | bytes 7864324
  211.4 109.9 %all-gather.8.cloned.1.call-start = ((), (), s32[]{:S(2)}) async-start(), calls=%async_computation.7 | async-start | bytes 6266880 | tf_op jit(solution)/shard_map/all_gather | solution.py:105
  220.0 2.8 copy-start.11
  222.4 1.8 copy-start.9
  222.9 2.2 copy-start.4
  224.2 1.9 copy-start.5
  225.0 1.9 copy-start.6
  226.1 1.9 copy-start.7
  226.9 1.9 copy-start.8
  229.3 94.7 %copy-start.1 = (bf16[16,3,3,16,80]{4,3,2,1,0:T(8,128)(2,1)S(1)}, bf16[16,3,3,16,80]{4,3,2,1,0:T(8,128)(2,1)}, u32[]{:S(2)}) copy-start(bf16[16,3,3,16,80]{4,3,2,1,0:T(8,128)(2,1)} %param.11) | copy-start | bytes 1105924
Sparse Core Ops, SparseCore 0:
  10.6 40.1 all-gather.5
  207.3 11.8 reduce-scatter.1
  221.5 37.6 all-gather.9
  261.9 59.3 all-gather.7
where the time goes:
time: 336 us; the launch traced here: 331 us
  waiting for transfers between devices  130 us (39%)
  local copies, waits for them, and re-layouts  92.5 us (28%)
  matrix products  46.2 us (14%)
  starting transfers between devices  23.9 us (7%)
  blocking collectives  17.2 us (5%)
  between operations  15.8 us (5%)
  other arithmetic  5.03 us (1%)
    all_gather x1, waiting for transfers between devices, local(): lax.all_gather(down_term[None], 'ten', axis=0, tiled=True)  60.2 us
    slice x9, local copies, waits for them, and re-layouts, local(): padded[tap_row:tap_row + height, tap_col:tap_col + breadth]  36.9 us
    conv_general_dilated x2, matrix products, conv_same(): lax.conv_general_dilated(field, kernel, (1, 1), 'SAME', dimension_numbers...  36.1 us
    all_gather x1, waiting for transfers between devices, local(): lax.all_gather(up_all[None, None, None], 'ten', axis=0, tiled=True)  29 us
    unnamed x56, local copies, waits for them, and re-layouts  23.9 us
    all_to_all x1, waiting for transfers between devices, local(): lax.all_to_all(y_cols, 'fsdp', split_axis=1, concat_axis=3, tiled=True)  14.7 us
    all_to_all x1, waiting for transfers between devices, local(): lax.all_to_all(send_down, 'ten', split_axis=0, concat_axis=4, tiled=True)  14.7 us
    all_to_all x1, starting transfers between devices, local(): lax.all_to_all(send_up, 'ten', split_axis=0, concat_axis=4, tiled=True)  8.46 us
  transfers between devices with their start and end apart: 8, of which 6 were waited for; matrix products, arithmetic and copies ran while one was open for 17% of the time, Pallas kernels for 0%

commit v1 on v0

--- a/solution.py
+++ b/solution.py
@@ -97,25 +97,10 @@
         rows_list.append(jnp.stack(cols_list))
     down_term = jnp.stack(rows_list).astype(jnp.bfloat16)
     up_all = lax.all_gather(up_term, "fsdp", axis=1, tiled=True)
-    start_buffers = (
-        jnp.zeros((groups,) + down_term.shape[:3] + (block_cols,), jnp.bfloat16),
-        jnp.zeros((groups, 1, 1, rank, block_cols), jnp.bfloat16),
-    )
-    down_piece = lax.dynamic_slice_in_dim(
-        lax.all_gather(down_term[None], "ten", axis=0, tiled=True),
-        ten_index * block_cols,
-        block_cols,
-        4,
-    )
-    up_piece = lax.dynamic_slice_in_dim(
-        lax.all_gather(up_all[None, None, None], "ten", axis=0, tiled=True),
-        ten_index * block_cols,
-        block_cols,
-        4,
-    )
-    up_new = lax.dynamic_update_slice_in_dim(start_buffers[1], up_piece, jnp.int32(0), 0)
+    down_piece = lax.all_to_all(down_term[None], "ten", split_axis=4, concat_axis=0, tiled=True)
+    up_piece = lax.all_to_all(up_all[None], "ten", split_axis=2, concat_axis=0, tiled=True)
     down_sum = jnp.einsum("dl,dabkc->labkc", picks, down_piece, preferred_element_type=jnp.float32)
-    up_sum = jnp.einsum("dl,dkc->lkc", picks, up_new[:, 0, 0], preferred_element_type=jnp.float32)
+    up_sum = jnp.einsum("dl,dkc->lkc", picks, up_piece, preferred_element_type=jnp.float32)
     return (block_out, down_sum.astype(jnp.bfloat16), up_sum.astype(jnp.bfloat16))
 
 

time: 336 us -> 293 us (0.87)
  the two profiles are of different devices: /device:TPU:11 before, /device:TPU:0 now
where the time goes in v1:
time: 293 us; the launch traced here: 289 us
  local copies, waits for them, and re-layouts  115 us (39%)
  waiting for transfers between devices  47.1 us (16%)
  matrix products  45.8 us (16%)
  starting transfers between devices  27.2 us (9%)
  blocking collectives  24.6 us (8%)
  between operations  16.1 us (5%)
  other arithmetic  12.7 us (4%)
    unnamed x61, local copies, waits for them, and re-layouts  38.6 us
    slice x9, local copies, waits for them, and re-layouts, local(): padded[tap_row:tap_row + height, tap_col:tap_col + breadth]  36.8 us
    conv_general_dilated x2, matrix products, conv_same(): lax.conv_general_dilated(field, kernel, (1, 1), 'SAME', dimension_numbers...  35.8 us
    all_to_all x1, waiting for transfers between devices, local(): lax.all_to_all(y_cols, 'fsdp', split_axis=1, concat_axis=3, tiled=True)  15.3 us
    all_to_all x1, waiting for transfers between devices, local(): lax.all_to_all(send_down, 'ten', split_axis=0, concat_axis=4, tiled=True)  15.2 us
    unnamed x1, blocking collectives  13.7 us
    all_to_all x1, waiting for transfers between devices, local(): lax.all_to_all(down_term[None], 'ten', split_axis=4, concat_axis=0, tiled...  9.95 us
    unnamed x1, other arithmetic  8.41 us
  transfers between devices with their start and end apart: 8, of which 4 were waited for; matrix products, arithmetic and copies ran while one was open for 26% of the time, Pallas kernels for 0%

profile of v1, /device:TPU:0, one launch (start us, length us, event | category | flops | bytes accessed | tf_op | source)
XLA Modules:
  0.0 288.7 jit_solution(12675517995085551883)
XLA Ops:
  7.3 3.2 %copy.127 = bf16[1,16,32,1280]{3,1,2,0:T(8,128)(2,1)} copy(bf16[1,16,32,1280]{3,2,1,0:T(8,128)(2,1)} %param.8) | data formatting | bytes 2621440 | tf_op args[0]
  11.1 0.6 dynamic-slice
  11.7 0.8 dynamic-update-slice
  12.5 13.7 %all-reduce.1 = s32[16]{0:T(128)S(1)} all-reduce(s32[16]{0:T(128)S(1)} %dynamic-update-slice), channel_id=1, replica_groups=mesh['ten'=16,'fsdp'=2] {'ten'}, use_global_device_ids=true, to_apply=%add.1 | all-reduce | flops 16 | bytes 128
  26.2 0.7 gather_fusion
  27.1 0.7 copy.140
  27.8 3.5 %all-to-all-start.1 = ((bf16[16,1,1,32,80]{4,3,2,1,0:T(8,128)(2,1)}), bf16[16,1,1,32,80]{4,3,2,1,0:T(8,128)(2,1)S(1)}, u32[]{:S(2)}, u32[]{:S(2)}) async-start(bf16[16,1,1,32,80]{4,3,2,1,0:T(8,128)(2,1)} %copy.140), calls=%async_computation.1 | async-start | bytes 262144 | tf_op jit(solution)/shard_map/all_to_all | solution.py:51
  31.7 1.0 copy.134
  32.7 6.5 %all-to-all-done.1 = bf16[16,1,1,32,80]{4,3,2,1,0:T(8,128)(2,1)S(1)} async-done(((bf16[16,1,1,32,80]{4,3,2,1,0:T(8,128)(2,1)}), bf16[16,1,1,32,80]{4,3,2,1,0:T(8,128)(2,1)S(1)}, u32[]{:S(2)}, u32[]{:S(2)}) %all-to-all-start.1) | async-done | bytes 81952 | tf_op jit(solution)/shard_map/all_to_all | solution.py:51
  39.2 3.8 %all-to-all-start = ((bf16[16,3,3,16,80]{4,3,2,1,0:T(8,128)(2,1)}), bf16[16,3,3,16,80]{4,3,2,1,0:T(8,128)(2,1)S(1)}, u32[]{:S(2)}, u32[]{:S(2)}) async-start(bf16[16,3,3,16,80]{4,3,2,1,0:T(8,128)(2,1)} %copy.134), calls=%async_computation | async-start | bytes 1179648 | tf_op jit(solution)/shard_map/all_to_all | solution.py:50
  43.2 15.2 %all-to-all-done = bf16[16,3,3,16,80]{4,3,2,1,0:T(8,128)(2,1)S(1)} async-done(((bf16[16,3,3,16,80]{4,3,2,1,0:T(8,128)(2,1)}), bf16[16,3,3,16,80]{4,3,2,1,0:T(8,128)(2,1)S(1)}, u32[]{:S(2)}, u32[]{:S(2)}) %all-to-all-start) | async-done | bytes 368672 | tf_op jit(solution)/shard_map/all_to_all | solution.py:50
  58.6 0.6 squeeze.10
  59.2 2.1 pad.5
  61.3 1.8 copy.129
  63.4 1.4 copy-done.18
  64.8 7.8 %fusion.19 = bf16[32,8,5,16]{3,1,2,0:T(8,128)(2,1)S(1)} fusion(bf16[3,3,16,1280]{3,2,1,0:T(8,128)(2,1)S(1)} %squeeze.10, bf16[32,1,7,2,1280]{4,2,3,0,1:T(8,128)(2,1)S(1)} %slice.39, bf16[32,1,8,5,1280]{4,2,3,0,1:T(8,128)(2,1)S(1)} %copy.129), kind=kOutput, calls=%fused_computation.42 | convolution fusion | flops 475791360 | bytes 4833280 | tf_op jit(solution)/shard_map/conv_general_dilated | solution.py:8
  73.0 28.0 %select_convert_fusion = bf16[32,8,5,640]{3,1,2,0:T(8,128)(2,1)S(1)} fusion(bf16[3,640,3,1280]{3,1,2,0:T(8,128)(2,1)} %param.10, bf16[32,1,7,2,1280]{4,2,3,0,1:T(8,128)(2,1)S(1)} %slice.39, bf16[32,1,8,5,1280]{4,2,3,0,1:T(8,128)(2,1)} %copy-done.18, pred[8,5]{0,1:T(8,128)(4,1)S(1)} %copy-done.23), kind=kOutput, calls=%fused_computation.13 | convolution fusion | flops 18496552960 | bytes 20807720 | tf_op jit(solution)/shard_map/conv_general_dilated | solution.py:8
  101.2 6.1 %all-gather = bf16[32,1,32,32]{0,3,2,1:T(8,128)(2,1)S(1)} all-gather(bf16[32,1,32,16]{0,3,2,1:T(8,128)(2,1)S(1)} %slice.41), channel_id=2, replica_groups=mesh['ten'=16,'fsdp'=2] {'fsdp'}, dimensions={3}, use_global_device_ids=true | all-gather | bytes 98304 | tf_op jit(solution)/shard_map/all_gather | solution.py:62
  108.2 1.5 copy.131
  109.8 1.6 fusion.9
  111.3 4.0 %all-to-all-start.2 = ((bf16[1,32,32,640]{3,2,0,1:T(8,128)(2,1)}), bf16[1,32,32,640]{3,2,0,1:T(8,128)(2,1)S(1)}, u32[]{:S(2)}, u32[]{:S(2)}) async-start(bf16[1,32,32,640]{3,2,0,1:T(8,128)(2,1)} %bitcast.15), calls=%async_computation.2 | async-start | bytes 2621440 | tf_op jit(solution)/shard_map/all_to_all | solution.py:68
  116.1 15.3 %all-to-all-done.2 = bf16[1,32,32,640]{3,2,0,1:T(8,128)(2,1)S(1)} async-done(((bf16[1,32,32,640]{3,2,0,1:T(8,128)(2,1)}), bf16[1,32,32,640]{3,2,0,1:T(8,128)(2,1)S(1)}, u32[]{:S(2)}, u32[]{:S(2)}) %all-to-all-start.2) | async-done | bytes 1310752 | tf_op jit(solution)/shard_map/all_to_all | solution.py:68
  131.4 1.3 copy.174
  132.7 0.9 all_to_all.81
  133.6 2.9 %fusion.8 = bf16[1,16,32,1280]{3,2,1,0:T(8,128)(2,1)S(1)} fusion(bf16[1,16,32,1280]{3,2,1,0:T(8,128)(2,1)S(1)} %all_to_all.81, bf16[1,16,32,1280]{3,2,1,0:T(8,128)(2,1)} %param.9, f32[]{:T(128)} %bitcast.20), kind=kLoop, calls=%fused_computation.21 | loop fusion | flops 7864320 | bytes 3932164 | tf_op jit(solution)/shard_map/convert_element_type | solution.py:21
  136.5 5.7 %copy.144 = bf16[1,16,32,1280]{2,1,0,3:T(8,128)(2,1)} copy(bf16[1,16,32,1280]{3,2,1,0:T(8,128)(2,1)S(1)} %fusion.8) | data formatting | bytes 2621440 | tf_op jit(solution)/shard_map/convert_element_type | solution.py:21
  142.2 7.7 %reshape.212 = bf16[2,2,163840]{2,1,0:T(2,128)(2,1)} reshape(bf16[1280,1,16,32]{3,2,1,0:T(8,128)(2,1)} %bitcast.130) | data formatting | bytes 2621440
  149.9 4.8 %all-to-all-start.3 = ((bf16[2,2,163840]{2,1,0:T(2,128)(2,1)}), bf16[2,2,163840]{2,1,0:T(2,128)(2,1)}, u32[]{:S(2)}, u32[]{:S(2)}) async-start(bf16[2,2,163840]{2,1,0:T(2,128)(2,1)} %reshape.212), calls=%async_computation.3 | async-start | bytes 2621440 | tf_op jit(solution)/shard_map/all_to_all | solution.py:70
  154.8 11.0 %pad_slice_fusion.7 = (bf16[32,32,1280]{2,0,1:T(8,128)(2,1)}, bf16[32,32,1280]{2,0,1:T(8,128)(2,1)}, bf16[32,32,1280]{2,0,1:T(8,128)(2,1)}, bf16[32,32,1280]{2,0...) fusion(bf16[32,32,1280]{2,0,1:T(8,128)(2,1)S(1)} %bitcast.129), kind=kLoop, calls=%fused_computation.12 | loop fusion | bytes 23592960 | tf_op jit(solution)/shard_map/slice | solution.py:89
  165.8 4.8 %copy.147 = bf16[32,32,1280]{2,1,0:T(8,128)(2,1)} copy(bf16[32,32,1280]{2,0,1:T(8,128)(2,1)} %get-tuple-element.21) | data formatting | bytes 5242880 | tf_op jit(solution)/shard_map/slice | solution.py:89
  170.7 3.0 %copy.148 = bf16[32,32,1280]{2,1,0:T(8,128)(2,1)} copy(bf16[32,32,1280]{2,0,1:T(8,128)(2,1)S(1)} %copy-done.17) | data formatting | bytes 5242880 | tf_op jit(solution)/shard_map/slice | solution.py:89
  173.7 3.0 %copy.149 = bf16[32,32,1280]{2,1,0:T(8,128)(2,1)} copy(bf16[32,32,1280]{2,0,1:T(8,128)(2,1)S(1)} %copy-done.16) | data formatting | bytes 5242880 | tf_op jit(solution)/shard_map/slice | solution.py:89
  176.7 2.9 %copy.150 = bf16[32,32,1280]{2,1,0:T(8,128)(2,1)} copy(bf16[32,32,1280]{2,0,1:T(8,128)(2,1)S(1)} %copy-done.15) | data formatting | bytes 5242880 | tf_op jit(solution)/shard_map/slice | solution.py:89
  179.6 2.9 %copy.152 = bf16[32,32,1280]{2,1,0:T(8,128)(2,1)} copy(bf16[32,32,1280]{2,0,1:T(8,128)(2,1)S(1)} %copy-done.14) | data formatting | bytes 5242880 | tf_op jit(solution)/shard_map/slice | solution.py:89
  182.5 2.9 %copy.153 = bf16[32,32,1280]{2,1,0:T(8,128)(2,1)} copy(bf16[32,32,1280]{2,0,1:T(8,128)(2,1)S(1)} %copy-done.13) | data formatting | bytes 5242880 | tf_op jit(solution)/shard_map/slice | solution.py:89
  185.5 3.0 %copy.154 = bf16[32,32,1280]{2,1,0:T(8,128)(2,1)} copy(bf16[32,32,1280]{2,0,1:T(8,128)(2,1)S(1)} %copy-done.12) | data formatting | bytes 5242880 | tf_op jit(solution)/shard_map/slice | solution.py:89
  188.5 3.2 %copy.155 = bf16[32,32,1280]{2,1,0:T(8,128)(2,1)} copy(bf16[32,32,1280]{2,0,1:T(8,128)(2,1)S(1)} %get-tuple-element.28) | data formatting | bytes 5242880 | tf_op jit(solution)/shard_map/slice | solution.py:89
  191.6 2.9 %copy.151 = bf16[1,32,32,1280]{3,2,1,0:T(8,128)(2,1)} copy(bf16[1,32,32,1280]{3,1,2,0:T(8,128)(2,1)S(1)} %copy-done.3) | data formatting | bytes 5242880 | tf_op jit(solution)/shard_map/all_gather | solution.py:56
  194.5 5.3 %reshape.213 = bf16[1280,1,16,32]{3,2,1,0:T(8,128)(2,1)} reshape(bf16[2,2,163840]{2,1,0:T(2,128)(2,1)} %all-to-all-done.3) | data formatting | bytes 2621440
  199.9 8.1 %copy.167 = bf16[1,16,32,2,640]{4,3,2,1,0:T(2,128)(2,1)S(1)} copy(bf16[1,16,32,2,640]{2,1,4,3,0:T(8,128)(2,1)} %bitcast.131) | data formatting | bytes 2621440 | tf_op jit(solution)/shard_map/all_to_all | solution.py:70
  208.2 1.2 fusion.27
  209.7 4.8 %all_gather.15 = bf16[32,1280]{1,0:T(8,128)(2,1)S(1)} all-gather(bf16[32,640]{1,0:T(8,128)(2,1)S(1)} %convolution_convert_fusion.13), channel_id=1, replica_groups=mesh['ten'=16,'fsdp'=2] {'fsdp'}, dimensions={1}, use_global_device_ids=true | all-gather | bytes 122880 | tf_op jit(solution)/shard_map/all_gather | solution.py:99
  214.5 1.2 copy.158
  215.7 0.5 broadcast.79
  216.2 8.4 %reduce = bf16[1280,32]{1,0:T(8,128)(2,1)S(1)} reduce(bf16[1280,1,32]{2,1,0:T(2,128)(2,1)} %bitcast.150, bf16[]{:T(256)} %broadcast.79), dimensions={1}, to_apply=%bitcast.101.reduce_sub_computation | reduce | bytes 163842
  224.6 0.9 reshape.216
  225.5 5.0 %all-to-all-start.5 = ((bf16[16,2,1280]{2,1,0:T(2,128)(2,1)}), bf16[16,2,1280]{2,1,0:T(2,128)(2,1)S(1)}, u32[]{:S(2)}, u32[]{:S(2)}) async-start(bf16[16,2,1280]{2,1,0:T(2,128)(2,1)} %reshape.216), calls=%async_computation.6 | async-start | bytes 163840 | tf_op jit(solution)/shard_map/all_to_all | solution.py:101
  230.6 0.8 convert_element_type.80
  231.4 2.3 fusion.14
  233.8 0.5 fusion.10
  234.2 0.5 fusion.11
  234.7 0.9 copy-done.6
  235.6 0.4 fusion.12
  236.4 0.4 fusion.13
  236.8 0.6 copy-done.8
  238.7 0.7 copy-done.10
  240.8 4.0 %copy.156 = bf16[1,3,3,16,1280]{3,2,1,0,4:T(4,128)(2,1)} copy(bf16[1,3,3,16,1280]{4,3,2,1,0:T(8,128)(2,1)S(1)} %pad_maximum_fusion) | data formatting | bytes 737280 | tf_op jit(solution)/shard_map/stack | solution.py:98
  244.7 7.4 %reshape.214 = bf16[16,2,5760]{2,1,0:T(2,128)(2,1)} reshape(bf16[1280,1,3,3,16]{4,3,2,1,0:T(4,128)(2,1)} %bitcast.132) | data formatting | bytes 737280
  252.1 6.0 %all-to-all-start.4 = ((bf16[16,2,5760]{2,1,0:T(2,128)(2,1)}), bf16[16,2,5760]{2,1,0:T(2,128)(2,1)S(1)}, u32[]{:S(2)}, u32[]{:S(2)}) async-start(bf16[16,2,5760]{2,1,0:T(2,128)(2,1)} %reshape.214), calls=%async_computation.5 | async-start | bytes 737280 | tf_op jit(solution)/shard_map/all_to_all | solution.py:100
  259.3 0.7 copy.161
  260.0 9.9 %all-to-all-done.4 = bf16[16,2,5760]{2,1,0:T(2,128)(2,1)S(1)} async-done(((bf16[16,2,5760]{2,1,0:T(2,128)(2,1)}), bf16[16,2,5760]{2,1,0:T(2,128)(2,1)S(1)}, u32[]{:S(2)}, u32[]{:S(2)}) %all-to-all-start.4) | async-done | bytes 368672 | tf_op jit(solution)/shard_map/all_to_all | solution.py:100
  269.9 5.6 %reshape.215 = bf16[1280,1,3,3,16]{4,3,2,1,0:T(4,128)(2,1)} reshape(bf16[16,2,5760]{2,1,0:T(2,128)(2,1)S(1)} %all-to-all-done.4) | data formatting | bytes 737280
  275.5 4.9 %copy.168 = bf16[1,3,3,16,16,80]{5,4,3,2,1,0:T(8,128)(2,1)S(1)} copy(bf16[1,3,3,16,16,80]{3,2,1,5,4,0:T(4,128)(2,1)} %bitcast.133) | data formatting | bytes 737280 | tf_op jit(solution)/shard_map/all_to_all | solution.py:100
  280.7 1.0 copy.160
  (82 shorter events, 7.9 us)
Async XLA Ops:
  7.2 24.1 %copy-start = (bf16[16,3,3,16,80]{4,3,2,1,0:T(8,128)(2,1)S(1)}, bf16[16,3,3,16,80]{4,3,2,1,0:T(8,128)(2,1)}, u32[]{:S(2)}) copy-start(bf16[16,3,3,16,80]{4,3,2,1,0:T(8,128)(2,1)} %param.11) | copy-start | bytes 1105924
  7.2 3.9 %copy-start.22 = (u32[32]{0:T(128)S(1)}, u32[32]{0:T(128)}, u32[]{:S(2)}) copy-start(u32[32]{0:T(128)} %constant.43) | copy-start | bytes 388
  7.2 19.0 %copy-start.2 = (s32[16]{0:T(128)S(1)}, s32[16]{0:T(128)}, u32[]{:S(2)}) copy-start(s32[16]{0:T(128)} %param.14) | copy-start | bytes 196
  7.2 19.6 %copy-start.20 = (bf16[16,32,80]{2,1,0:T(8,128)(2,1)S(1)}, bf16[16,32,80]{2,1,0:T(8,128)(2,1)}, u32[]{:S(2)}) copy-start(bf16[16,32,80]{2,1,0:T(8,128)(2,1)} %param.12) | copy-start | bytes 245764
  7.2 52.0 %all-gather.3.cloned.1.call-start = ((), (), s32[]{:S(2)}) async-start(), calls=%async_computation.7 | async-start | bytes 3932160 | tf_op jit(solution)/shard_map/all_gather | solution.py:56
  27.8 11.4 %all-to-all-start.1 = ((bf16[16,1,1,32,80]{4,3,2,1,0:T(8,128)(2,1)}), bf16[16,1,1,32,80]{4,3,2,1,0:T(8,128)(2,1)S(1)}, u32[]{:S(2)}, u32[]{:S(2)}) async-start(bf16[16,1,1,32,80]{4,3,2,1,0:T(8,128)(2,1)} %copy.140), calls=%async_computation.1 | async-start | bytes 262144 | tf_op jit(solution)/shard_map/all_to_all | solution.py:51
  39.2 19.3 %all-to-all-start = ((bf16[16,3,3,16,80]{4,3,2,1,0:T(8,128)(2,1)}), bf16[16,3,3,16,80]{4,3,2,1,0:T(8,128)(2,1)S(1)}, u32[]{:S(2)}, u32[]{:S(2)}) async-start(bf16[16,3,3,16,80]{4,3,2,1,0:T(8,128)(2,1)} %copy.134), calls=%async_computation | async-start | bytes 1179648 | tf_op jit(solution)/shard_map/all_to_all | solution.py:50
  63.1 1.7 copy-start.18
  64.8 8.1 %copy-start.21 = (pred[8,5]{1,0:T(8,128)(4,1)S(1)}, pred[8,5]{1,0:T(8,128)(4,1)}, u32[]{:S(2)}) copy-start(pred[8,5]{1,0:T(8,128)(4,1)} %constant.39) | copy-start | bytes 124
  64.8 8.2 %copy-start.23 = (pred[8,5]{0,1:T(8,128)(4,1)S(1)}, pred[8,5]{0,1:T(8,128)(4,1)}, u32[]{:S(2)}) copy-start(pred[8,5]{0,1:T(8,128)(4,1)} %constant.47) | copy-start | bytes 124
  111.3 20.0 %all-to-all-start.2 = ((bf16[1,32,32,640]{3,2,0,1:T(8,128)(2,1)}), bf16[1,32,32,640]{3,2,0,1:T(8,128)(2,1)S(1)}, u32[]{:S(2)}, u32[]{:S(2)}) async-start(bf16[1,32,32,640]{3,2,0,1:T(8,128)(2,1)} %bitcast.15), calls=%async_computation.2 | async-start | bytes 2621440 | tf_op jit(solution)/shard_map/all_to_all | solution.py:68
  133.6 8.6 %copy-start.19 = (bf16[1,16,32,1280]{3,2,1,0:T(8,128)(2,1)}, bf16[1,16,32,1280]{3,2,1,0:T(8,128)(2,1)S(1)}, u32[]{:S(2)}) copy-start(bf16[1,16,32,1280]{3,2,1,0:T(8,128)(2,1)S(1)} %all_to_all.81) | copy-start | bytes 3932164
  149.9 4.9 %copy-start.3 = (bf16[1,32,32,1280]{3,1,2,0:T(8,128)(2,1)S(1)}, bf16[1,32,32,1280]{3,1,2,0:T(8,128)(2,1)}, u32[]{:S(2)}) copy-start(bf16[1,32,32,1280]{3,1,2,0:T(8,128)(2,1)} %all-gather.3.cloned.1.call-done) | copy-start | bytes 7864324
  149.9 44.6 %all-to-all-start.3 = ((bf16[2,2,163840]{2,1,0:T(2,128)(2,1)}), bf16[2,2,163840]{2,1,0:T(2,128)(2,1)}, u32[]{:S(2)}, u32[]{:S(2)}) async-start(bf16[2,2,163840]{2,1,0:T(2,128)(2,1)} %reshape.212), calls=%async_computation.3 | async-start | bytes 2621440 | tf_op jit(solution)/shard_map/all_to_all | solution.py:70
  154.8 75.8 %reduce-scatter.2.cloned.1.call-start = ((), (), s32[]{:S(2)}) async-start(), calls=%async_computation.8 | async-start | bytes 196608 | tf_op jit(solution)/shard_map/reduce_scatter | solution.py:80
  165.8 4.8 %copy-start.17 = (bf16[32,32,1280]{2,0,1:T(8,128)(2,1)S(1)}, bf16[32,32,1280]{2,0,1:T(8,128)(2,1)}, u32[]{:S(2)}) copy-start(bf16[32,32,1280]{2,0,1:T(8,128)(2,1)} %get-tuple-element.22) | copy-start | bytes 7864324
  170.7 3.0 %copy-start.16 = (bf16[32,32,1280]{2,0,1:T(8,128)(2,1)S(1)}, bf16[32,32,1280]{2,0,1:T(8,128)(2,1)}, u32[]{:S(2)}) copy-start(bf16[32,32,1280]{2,0,1:T(8,128)(2,1)} %get-tuple-element.23) | copy-start | bytes 7864324
  173.7 3.0 %copy-start.15 = (bf16[32,32,1280]{2,0,1:T(8,128)(2,1)S(1)}, bf16[32,32,1280]{2,0,1:T(8,128)(2,1)}, u32[]{:S(2)}) copy-start(bf16[32,32,1280]{2,0,1:T(8,128)(2,1)} %get-tuple-element.24) | copy-start | bytes 7864324
  176.7 2.9 %copy-start.14 = (bf16[32,32,1280]{2,0,1:T(8,128)(2,1)S(1)}, bf16[32,32,1280]{2,0,1:T(8,128)(2,1)}, u32[]{:S(2)}) copy-start(bf16[32,32,1280]{2,0,1:T(8,128)(2,1)} %get-tuple-element.25) | copy-start | bytes 7864324
  179.6 2.9 %copy-start.13 = (bf16[32,32,1280]{2,0,1:T(8,128)(2,1)S(1)}, bf16[32,32,1280]{2,0,1:T(8,128)(2,1)}, u32[]{:S(2)}) copy-start(bf16[32,32,1280]{2,0,1:T(8,128)(2,1)} %get-tuple-element.26) | copy-start | bytes 7864324
  182.5 2.9 %copy-start.12 = (bf16[32,32,1280]{2,0,1:T(8,128)(2,1)S(1)}, bf16[32,32,1280]{2,0,1:T(8,128)(2,1)}, u32[]{:S(2)}) copy-start(bf16[32,32,1280]{2,0,1:T(8,128)(2,1)} %get-tuple-element.27) | copy-start | bytes 7864324
  209.7 24.0 %copy-start.4 = (bf16[32,32,1280]{2,1,0:T(8,128)(2,1)S(1)}, bf16[32,32,1280]{2,1,0:T(8,128)(2,1)}, u32[]{:S(2)}) copy-start(bf16[32,32,1280]{2,1,0:T(8,128)(2,1)} %copy.147) | copy-start | bytes 7864324
  225.5 26.6 %all-to-all-start.5 = ((bf16[16,2,1280]{2,1,0:T(2,128)(2,1)}), bf16[16,2,1280]{2,1,0:T(2,128)(2,1)S(1)}, u32[]{:S(2)}, u32[]{:S(2)}) async-start(bf16[16,2,1280]{2,1,0:T(2,128)(2,1)} %reshape.216), calls=%async_computation.6 | async-start | bytes 163840 | tf_op jit(solution)/shard_map/all_to_all | solution.py:101
  231.4 2.8 copy-start.5
  233.8 1.8 copy-start.6
  234.2 2.2 copy-start.7
  235.5 1.9 copy-start.8
  236.4 1.9 copy-start.9
  237.5 1.9 copy-start.10
  238.3 1.9 copy-start.11
  252.1 17.8 %all-to-all-start.4 = ((bf16[16,2,5760]{2,1,0:T(2,128)(2,1)}), bf16[16,2,5760]{2,1,0:T(2,128)(2,1)S(1)}, u32[]{:S(2)}, u32[]{:S(2)}) async-start(bf16[16,2,5760]{2,1,0:T(2,128)(2,1)} %reshape.214), calls=%async_computation.5 | async-start | bytes 737280 | tf_op jit(solution)/shard_map/all_to_all | solution.py:100
  275.5 6.2 %copy-start.1 = (bf16[16,3,3,16,80]{4,3,2,1,0:T(8,128)(2,1)S(1)}, bf16[16,3,3,16,80]{4,3,2,1,0:T(8,128)(2,1)}, u32[]{:S(2)}) copy-start(bf16[16,3,3,16,80]{4,3,2,1,0:T(8,128)(2,1)} %param.11) | copy-start | bytes 1105924
Sparse Core Ops, SparseCore 0:
  10.6 41.7 all-gather.2
  209.5 10.9 reduce-scatter.1

commit v2 on v1

--- a/solution.py
+++ b/solution.py
@@ -1,6 +1,10 @@
+import functools
+
 import jax
 import jax.numpy as jnp
 from jax import lax
+from jax.experimental import pallas as pl
+from jax.experimental.pallas import tpu as pltpu
 from jax.sharding import PartitionSpec as P
 
 
@@ -104,6 +108,273 @@
     return (block_out, down_sum.astype(jnp.bfloat16), up_sum.astype(jnp.bfloat16))
 
 
+NT = (((1,), (1,)), ((), ()))
+TN = (((0,), (0,)), ((), ()))
+F32 = jnp.float32
+BF16 = jnp.bfloat16
+
+
+def core_kernel(
+    act, cot, kern, df, up, wgt, out, down_out, up_out,
+    field, kbuf, part, lown, lowp, bbuf, block, ysend, cotv, slope, lgt, lgall, taps, upp, upr,
+    ksem, lsem, ssem, rsem, *, wide, chunk,
+):
+    y = lax.axis_index("fsdp")
+    other = 1 - y
+    peer = {"fsdp": other}
+    cells, channels = act.shape
+    width = kern.shape[1]
+    half = df.shape[1]
+    total = 2 * cells
+
+    def rows(start, size):
+        return pl.ds(pl.multiple_of(start, wide), size)
+
+    ranks = pl.ds(pl.multiple_of(width + half * y, half), half)
+    mine = wide + cells * y
+    theirs = wide + cells * other
+
+    def send(src, dst, k):
+        return pltpu.make_async_remote_copy(
+            src_ref=src, dst_ref=dst, send_sem=ssem.at[k], recv_sem=rsem.at[k],
+            device_id=peer, device_id_type=pl.DeviceIdType.MESH,
+        )
+
+    def tap_copy(t):
+        return pltpu.make_async_copy(kern.at[t], kbuf.at[t, pl.ds(0, width)], ksem.at[t])
+
+    act_copy = pltpu.make_async_copy(act, field.at[rows(mine, cells)], lsem.at[0])
+    df_copy = pltpu.make_async_copy(df, kbuf.at[:, ranks], lsem.at[1])
+    act_copy.start()
+    df_copy.start()
+    for t in range(9):
+        tap_copy(t).start()
+    cot_copies = []
+    for h in range(2):
+        cot_copies.append(
+            pltpu.make_async_copy(
+                cot.at[:, pl.ds(h * width, width)], cotv.at[h], lsem.at[2 + h]
+            )
+        )
+        cot_copies[-1].start()
+
+    barrier = pltpu.get_barrier_semaphore()
+    pl.semaphore_signal(barrier, inc=1, device_id=peer, device_id_type=pl.DeviceIdType.MESH)
+    pl.semaphore_wait(barrier, 1)
+
+    far = cells - chunk - wide
+    spans = (
+        ((cells - wide) * other, wide),
+        (far * other + wide * y, chunk),
+        ((wide + chunk) * y, far),
+    )
+    df_send = send(df, kbuf.at[:, ranks], 0)
+    df_send.start()
+    moves = [
+        send(act.at[rows(start, size)], field.at[rows(mine + start, size)], 1 + n)
+        for n, (start, size) in enumerate(spans)
+    ]
+    for move in moves:
+        move.start()
+
+    field[pl.ds(0, wide), :] = jnp.zeros((wide, channels), BF16)
+    field[pl.ds(wide + total, wide), :] = jnp.zeros((wide, channels), BF16)
+    act_copy.wait()
+    df_copy.wait()
+    df_send.wait_recv()
+    moves[0].wait_recv()
+
+    def conv(first_cell, count, low, first):
+        part[:, pl.ds(0, count), :] = jnp.zeros((3, count, part.shape[2]), F32)
+
+        def tap(t, carry):
+            if first:
+                tap_copy(t).wait()
+            shifted = field[rows(first_cell + wide * (t // 3), count), :]
+            part[t % 3, pl.ds(0, count), :] += lax.dot_general(
+                shifted, kbuf[t], NT, preferred_element_type=F32
+            )
+            return carry
+
+        lax.fori_loop(0, 9, tap, 0)
+
+        def join(r, carry):
+            span = rows(r * wide, wide)
+            col = lax.broadcasted_iota(jnp.int32, (wide, part.shape[2]), 0)
+            whole = (
+                part[1, span, :]
+                + jnp.where(col > 0, pltpu.roll(part[0, span, :], 1, 0), 0.0)
+                + jnp.where(col < wide - 1, pltpu.roll(part[2, span, :], wide - 1, 0), 0.0)
+            )
+            bbuf[span, :] = whole[:, :width].astype(BF16)
+            low[span, :] = whole[:, width:].astype(BF16)
+            return carry
+
+        lax.fori_loop(0, count // wide, join, 0)
+
+    def finish(count, low):
+        return (
+            bbuf[pl.ds(0, count), :].astype(F32)
+            + jnp.dot(low[pl.ds(0, count), :], up[y], preferred_element_type=F32)
+        ).astype(BF16)
+
+    conv(cells * y, cells, lown, True)
+    block[y] = finish(cells, lown)
+
+    moves[1].wait_recv()
+    near = chunk * y
+    conv(cells * other + near, chunk, lowp, False)
+    ysend[rows(near, chunk), :] = finish(chunk, lowp)
+    near_send = send(ysend.at[rows(near, chunk)], block.at[y, rows(near, chunk)], 4)
+    near_send.start()
+
+    moves[2].wait_recv()
+    rest = chunk * other
+    conv(cells * other + rest, chunk, lowp, False)
+    ysend[rows(rest, chunk), :] = finish(chunk, lowp)
+    rest_send = send(ysend.at[rows(rest, chunk)], block.at[y, rows(rest, chunk)], 5)
+    rest_send.start()
+
+    for copy in cot_copies:
+        copy.wait()
+    weight = wgt[0]
+
+    def slopes(h, start, count):
+        def step(r, carry):
+            span = rows(start + r * wide, wide)
+            value = block[h, span, :].astype(F32)
+            sigma = jax.nn.sigmoid(value)
+            slope[h, span, :] = (
+                cotv[h, span, :].astype(F32) * weight * sigma * (1.0 + value * (1.0 - sigma))
+            ).astype(BF16)
+            return carry
+
+        lax.fori_loop(0, count // wide, step, 0)
+
+    slopes(y, 0, cells)
+    near_send.wait_recv()
+    slopes(other, chunk * other, chunk)
+    rest_send.wait_recv()
+    outs = [
+        pltpu.make_async_copy(block.at[h], out.at[:, pl.ds(h * width, width)], lsem.at[4 + h])
+        for h in range(2)
+    ]
+    for copy in outs:
+        copy.start()
+    slopes(other, chunk * y, chunk)
+
+    grad = lax.dot_general(up[0], slope[0], NT, preferred_element_type=F32) + lax.dot_general(
+        up[1], slope[1], NT, preferred_element_type=F32
+    )
+    lgt[...] = grad.astype(BF16)
+    lanes = pl.ds(pl.multiple_of(cells * y, 128), cells)
+    lg_send = send(lgt.at[pl.ds(pl.multiple_of(half * other, half), half)], lgall.at[:, lanes], 6)
+    lg_send.start()
+    for h in range(2):
+        upp[h] = lax.dot_general(lown[...], slope[h], TN, preferred_element_type=F32)
+    up_send = send(upp, upr, 7)
+    up_send.start()
+    lgall[:, lanes] = lgt[pl.ds(pl.multiple_of(half * y, half), half), :]
+    lg_send.wait_recv()
+
+    grads = lgall[...].astype(F32)
+    place = lax.broadcasted_iota(jnp.int32, (half, total), 1)
+    row, col = place // wide, place % wide
+    high = total // wide
+    for t in range(9):
+        da, db = t // 3 - 1, t % 3 - 1
+        offset = (da * wide + db) % total
+        moved = pltpu.roll(grads, offset, 1) if offset else grads
+        inside = (row >= da) & (row < high + da) & (col >= db) & (col < wide + db)
+        taps[pl.ds(t * half, half), :] = jnp.where(inside, moved, 0.0).astype(BF16)
+    down_out[...] = jnp.dot(
+        taps[...], field[pl.ds(wide, total), :], preferred_element_type=F32
+    ).astype(BF16)
+    up_send.wait_recv()
+    for h in range(2):
+        up_out[:, pl.ds(h * width, width)] = (upp[h] + upr[h]).astype(BF16)
+    for copy in [df_send, *moves, near_send, rest_send, lg_send, up_send]:
+        copy.wait_send()
+    for copy in outs:
+        copy.wait()
+
+
+def local_pair(
+    activations, cotangent, base_kernel, down_table, up_table, sample_tenant, tenant_slot, timesteps
+):
+    width = base_kernel.shape[1]
+    _, height, wide, channels = activations.shape
+    cells = height * wide
+    chunk = cells // 2
+    tenants, _, _, half, block_cols = down_table.shape
+    rank = up_table.shape[1]
+    kernel_taps = jnp.transpose(base_kernel, (0, 2, 1, 3)).reshape(9, width, channels)
+    all_tenants = lax.all_gather(sample_tenant, "ten", axis=0, tiled=True)
+    all_slots = tenant_slot[all_tenants]
+    groups = all_slots.shape[0]
+    picks = (all_slots[:, None] == jnp.arange(tenants, dtype=jnp.int32)[None, :]).astype(BF16)
+    table = jnp.concatenate([down_table.reshape(tenants, 9 * half, block_cols), up_table], axis=1)
+    sent = jnp.einsum("dl,lkc->dkc", picks, table, preferred_element_type=F32).astype(BF16)
+    factors = lax.all_to_all(sent, "ten", split_axis=0, concat_axis=0, tiled=True)
+    factors = jnp.transpose(factors, (1, 0, 2)).reshape(9 * half + rank, channels)
+    df = factors[: 9 * half].reshape(9, half, channels)
+    up = jnp.transpose(factors[9 * half :].reshape(rank, 2, width), (1, 0, 2))
+    weight = 1.0 / (1.0 + timesteps.astype(F32) / 250.0)
+
+    anywhere = pl.BlockSpec(memory_space=pl.ANY)
+    vmem = pl.BlockSpec(memory_space=pltpu.VMEM)
+    block_out, down_term, up_term = pl.pallas_call(
+        functools.partial(core_kernel, wide=wide, chunk=chunk),
+        out_shape=(
+            jax.ShapeDtypeStruct((cells, channels), BF16),
+            jax.ShapeDtypeStruct((9 * half, channels), BF16),
+            jax.ShapeDtypeStruct((rank, channels), BF16),
+        ),
+        in_specs=[anywhere] * 4 + [vmem, pl.BlockSpec(memory_space=pltpu.SMEM)],
+        out_specs=(anywhere, vmem, vmem),
+        scratch_shapes=[
+            pltpu.VMEM((2 * cells + 2 * wide, channels), BF16),
+            pltpu.VMEM((9, width + rank, channels), BF16),
+            pltpu.VMEM((3, cells, width + rank), F32),
+            pltpu.VMEM((cells, rank), BF16),
+            pltpu.VMEM((chunk, rank), BF16),
+            pltpu.VMEM((cells, width), BF16),
+            pltpu.VMEM((2, cells, width), BF16),
+            pltpu.VMEM((cells, width), BF16),
+            pltpu.VMEM((2, cells, width), BF16),
+            pltpu.VMEM((2, cells, width), BF16),
+            pltpu.VMEM((rank, cells), BF16),
+            pltpu.VMEM((half, 2 * cells), BF16),
+            pltpu.VMEM((9 * half, 2 * cells), BF16),
+            pltpu.VMEM((2, rank, width), F32),
+            pltpu.VMEM((2, rank, width), F32),
+            pltpu.SemaphoreType.DMA((9,)),
+            pltpu.SemaphoreType.DMA((6,)),
+            pltpu.SemaphoreType.DMA((8,)),
+            pltpu.SemaphoreType.DMA((8,)),
+        ],
+        compiler_params=pltpu.CompilerParams(
+            collective_id=0, has_side_effects=True, vmem_limit_bytes=56 * 1024 * 1024
+        ),
+    )(
+        activations.reshape(cells, channels),
+        cotangent.reshape(cells, channels),
+        kernel_taps,
+        df,
+        up,
+        weight,
+    )
+    terms = jnp.concatenate([down_term, up_term], axis=0).reshape(-1, groups, block_cols)
+    terms = jnp.transpose(terms, (1, 0, 2))
+    pieces = lax.all_to_all(terms, "ten", split_axis=0, concat_axis=0, tiled=True)
+    sums = jnp.einsum("dl,dkc->lkc", picks, pieces, preferred_element_type=F32).astype(BF16)
+    return (
+        block_out.reshape(activations.shape),
+        sums[:, : 9 * half].reshape(down_table.shape),
+        sums[:, 9 * half :],
+    )
+
+
 def solution(mesh):
     placed = (
         P("ten", "fsdp", None, None),
@@ -116,7 +387,7 @@
         P("ten"),
     )
     return jax.shard_map(
-        local,
+        local_pair if mesh.shape["fsdp"] == 2 else local,
         mesh=mesh,
         in_specs=placed,
         out_specs=(

time: 293 us -> 137 us (0.47)
  the two profiles are of different devices: /device:TPU:0 before, /device:TPU:11 now
where the time goes in v2:
time: 137 us; the launch traced here: 135 us
  Pallas kernels  59 us (43%)
  waiting for transfers between devices  32.2 us (24%)
  starting transfers between devices  16.4 us (12%)
  local copies, waits for them, and re-layouts  15.8 us (12%)
  blocking collectives  7.86 us (6%)
  between operations  2.08 us (2%)
    pallas_call x1, Pallas kernels, local_pair(): pl.pallas_call(functools.partial(core_kernel, wide=wide, chunk=chunk), ou...  59 us
    all_to_all x1, waiting for transfers between devices, local_pair(): lax.all_to_all(terms, 'ten', split_axis=0, concat_axis=0, tiled=True)  16.4 us
    all_to_all x1, waiting for transfers between devices, local_pair(): lax.all_to_all(sent, 'ten', split_axis=0, concat_axis=0, tiled=True)  15.8 us
    all_to_all x1, starting transfers between devices, local_pair(): lax.all_to_all(sent, 'ten', split_axis=0, concat_axis=0, tiled=True)  8.54 us
    all_to_all x1, starting transfers between devices, local_pair(): lax.all_to_all(terms, 'ten', split_axis=0, concat_axis=0, tiled=True)  7.87 us
    unnamed x1, blocking collectives  7.86 us
    unnamed x10, local copies, waits for them, and re-layouts  5.22 us
  transfers between devices with their start and end apart: 2, of which 2 were waited for; matrix products, arithmetic and copies ran while one was open for 0% of the time, Pallas kernels for 0%

profile of v2, /device:TPU:11, one launch (start us, length us, event | category | flops | bytes accessed | tf_op | source)
XLA Modules:
  0.0 135.2 jit_solution(3341496620092782458)
XLA Ops:
  0.6 0.0 copy-start
  1.3 1.2 dynamic-slice
  2.6 0.8 dynamic-update-slice
  3.3 7.9 %all-reduce = s32[16]{0:T(128)S(1)} all-reduce(s32[16]{0:T(128)S(1)} %dynamic-update-slice), channel_id=1, replica_groups=mesh['ten'=16,'fsdp'=2] {'ten'}, use_global_device_ids=true, to_apply=%add | all-reduce | flops 16 | bytes 128
  11.2 1.2 copy.28
  12.4 1.9 %copy.27 = bf16[16,144,80]{1,0,2:T(8,128)(2,1)S(1)} copy(bf16[16,144,80]{2,1,0:T(8,128)(2,1)} %bitcast.29) | data formatting | bytes 737280 | tf_op jit(solution)/shard_map/reshape | solution.py:316
  14.3 0.0 copy-done
  14.3 0.7 gather_fusion
  15.0 0.4 convolution_convert_fusion.1
  15.4 1.0 copy.30
  16.4 8.5 %all-to-all-start = ((bf16[16,176,80]{1,2,0:T(8,128)(2,1)}), bf16[16,176,80]{1,2,0:T(8,128)(2,1)S(1)}, u32[]{:S(2)}, u32[]{:S(2)}) async-start(bf16[16,176,80]{1,2,0:T(8,128)(2,1)} %copy.30), calls=%async_computation | async-start | bytes 1310720 | tf_op jit(solution)/shard_map/all_to_all | solution.py:318
  25.7 15.8 %all-to-all-done = bf16[16,176,80]{1,2,0:T(8,128)(2,1)S(1)} async-done(((bf16[16,176,80]{1,2,0:T(8,128)(2,1)}), bf16[16,176,80]{1,2,0:T(8,128)(2,1)S(1)}, u32[]{:S(2)}, u32[]{:S(2)}) %all-to-all-start) | async-done | bytes 450592 | tf_op jit(solution)/shard_map/all_to_all | solution.py:318
  41.4 0.2 slice.21
  41.6 0.8 copy.33
  42.4 0.5 copy.31
  42.9 1.3 reshape.43.df
  44.2 59.0 %shard_map.103 = (bf16[512,1280]{1,0:T(8,128)(2,1)}, bf16[144,1280]{1,0:T(8,128)(2,1)}, bf16[32,1280]{1,0:T(8,128)(2,1)}) custom-call(bf16[512,1280]{1,0:T(8,128)(2,1)} %bitcast.25, bf16[512,1280]{1,0:T(8,128)(2,1)} %bitcast.26, bf16[9,640,1280]{2,1,0:T(8,128)(2,1)} %bitcast.20, bf16[9,16,1280]{2,1,0:T(8,128)(2,1)} %reshape.43.df, ...), custom_call_target="tpu_custom_call" | custom-call | tf_op jit(solution)/shard_map/pallas_call | solution.py:326
  103.2 1.1 pad_maximum_fusion
  104.3 1.1 reshape.46
  105.4 1.5 %copy.34 = bf16[16,176,80]{1,2,0:T(8,128)(2,1)} copy(bf16[16,176,80]{2,0,1:T(8,128)(2,1)S(1)} %bitcast.24) | data formatting | bytes 901120 | tf_op jit(solution)/shard_map/transpose | solution.py:368
  106.9 7.9 %all-to-all-start.1 = ((bf16[16,176,80]{1,2,0:T(8,128)(2,1)}), bf16[16,176,80]{1,2,0:T(8,128)(2,1)S(1)}, u32[]{:S(2)}, u32[]{:S(2)}) async-start(bf16[16,176,80]{1,2,0:T(8,128)(2,1)} %copy.34), calls=%async_computation.1 | async-start | bytes 1310720 | tf_op jit(solution)/shard_map/all_to_all | solution.py:369
  114.7 16.4 %all-to-all-done.1 = bf16[16,176,80]{1,2,0:T(8,128)(2,1)S(1)} async-done(((bf16[16,176,80]{1,2,0:T(8,128)(2,1)}), bf16[16,176,80]{1,2,0:T(8,128)(2,1)S(1)}, u32[]{:S(2)}, u32[]{:S(2)}) %all-to-all-start.1) | async-done | bytes 450592 | tf_op jit(solution)/shard_map/all_to_all | solution.py:369
  131.2 0.3 convolution_convert_fusion
  131.5 0.0 copy-start.1
  131.5 0.2 slice.23
  131.7 1.0 copy.37
  132.6 1.5 %copy.36 = bf16[16,144,80]{2,1,0:T(8,128)(2,1)} copy(bf16[16,144,80]{1,0,2:T(8,128)(2,1)S(1)} %bitcast.23) | data formatting | bytes 737280 | tf_op jit(solution)/shard_map/slice | solution.py:373
  134.1 0.0 copy-done.1
  134.1 1.1 copy.48
  (3 shorter events, 0.0 us)
Async XLA Ops:
  0.6 13.7 %copy-start = (s32[16]{0:T(128)S(1)}, s32[16]{0:T(128)}, u32[]{:S(2)}) copy-start(s32[16]{0:T(128)} %param.14) | copy-start | bytes 196
  16.4 25.0 %all-to-all-start = ((bf16[16,176,80]{1,2,0:T(8,128)(2,1)}), bf16[16,176,80]{1,2,0:T(8,128)(2,1)S(1)}, u32[]{:S(2)}, u32[]{:S(2)}) async-start(bf16[16,176,80]{1,2,0:T(8,128)(2,1)} %copy.30), calls=%async_computation | async-start | bytes 1310720 | tf_op jit(solution)/shard_map/all_to_all | solution.py:318
  106.9 24.3 %all-to-all-start.1 = ((bf16[16,176,80]{1,2,0:T(8,128)(2,1)}), bf16[16,176,80]{1,2,0:T(8,128)(2,1)S(1)}, u32[]{:S(2)}, u32[]{:S(2)}) async-start(bf16[16,176,80]{1,2,0:T(8,128)(2,1)} %copy.34), calls=%async_computation.1 | async-start | bytes 1310720 | tf_op jit(solution)/shard_map/all_to_all | solution.py:369
  131.5 2.6 %copy-start.1 = (bf16[512,1280]{1,0:T(8,128)(2,1)S(1)}, bf16[512,1280]{1,0:T(8,128)(2,1)}, u32[]{:S(2)}) copy-start(bf16[512,1280]{1,0:T(8,128)(2,1)} %get-tuple-element.6) | copy-start | bytes 3932164

commit v3 on v2

--- a/solution.py
+++ b/solution.py
@@ -115,16 +115,21 @@
 
 
 def core_kernel(
-    act, cot, kern, df, up, wgt, out, down_out, up_out,
+    act, cot, kern, table, tenant, slot_of, wgt, out, pieces_out, slots_out,
+    slot_mine, slots, slots_s, fac_send, fac_recv, fac, fin, fin_recv, up,
     field, kbuf, part, lown, lowp, bbuf, block, ysend, cotv, slope, lgt, lgall, taps, upp, upr,
-    ksem, lsem, ssem, rsem, *, wide, chunk,
+    ksem, lsem, ssem, rsem, tsend, trecv, *, wide, chunk,
 ):
+    me = lax.axis_index("ten")
+    terms, block_cols = table.shape[1], table.shape[2]
+    groups = slots.shape[0]
     y = lax.axis_index("fsdp")
     other = 1 - y
     peer = {"fsdp": other}
     cells, channels = act.shape
     width = kern.shape[1]
-    half = df.shape[1]
+    half = lgall.shape[0]
+    rank = 2 * half
     total = 2 * cells
 
     def rows(start, size):
@@ -144,9 +149,7 @@
         return pltpu.make_async_copy(kern.at[t], kbuf.at[t, pl.ds(0, width)], ksem.at[t])
 
     act_copy = pltpu.make_async_copy(act, field.at[rows(mine, cells)], lsem.at[0])
-    df_copy = pltpu.make_async_copy(df, kbuf.at[:, ranks], lsem.at[1])
     act_copy.start()
-    df_copy.start()
     for t in range(9):
         tap_copy(t).start()
     cot_copies = []
@@ -158,9 +161,40 @@
         )
         cot_copies[-1].start()
 
+    def ten_copy(src, dst, kind, k, source):
+        return pltpu.make_async_remote_copy(
+            src_ref=src, dst_ref=dst, send_sem=tsend.at[kind, k], recv_sem=trecv.at[kind, source],
+            device_id={"ten": lax.rem(me + k, groups)}, device_id_type=pl.DeviceIdType.MESH,
+        )
+
+    def each_other(body):
+        def step(k, carry):
+            body(k)
+            return carry
+
+        lax.fori_loop(1, groups, step, 0)
+
+    def arrived(src, dst, kind):
+        def body(k):
+            source = lax.rem(me + k, groups)
+            ten_copy(src.at[source], dst.at[source], kind, k, source).wait_recv()
+
+        each_other(body)
+
+    slot_mine[...] = jnp.full(slot_mine.shape, slot_of[tenant[0]], jnp.int32)
+    slots[me] = slot_mine[0]
     barrier = pltpu.get_barrier_semaphore()
     pl.semaphore_signal(barrier, inc=1, device_id=peer, device_id_type=pl.DeviceIdType.MESH)
-    pl.semaphore_wait(barrier, 1)
+
+    def greet(k):
+        pl.semaphore_signal(
+            barrier, inc=1, device_id={"ten": lax.rem(me + k, groups)},
+            device_id_type=pl.DeviceIdType.MESH,
+        )
+
+    each_other(greet)
+    pl.semaphore_wait(barrier, groups)
+    each_other(lambda k: ten_copy(slot_mine.at[0], slots.at[me], 0, k, me).start())
 
     far = cells - chunk - wide
     spans = (
@@ -168,8 +202,6 @@
         (far * other + wide * y, chunk),
         ((wide + chunk) * y, far),
     )
-    df_send = send(df, kbuf.at[:, ranks], 0)
-    df_send.start()
     moves = [
         send(act.at[rows(start, size)], field.at[rows(mine + start, size)], 1 + n)
         for n, (start, size) in enumerate(spans)
@@ -179,25 +211,42 @@
 
     field[pl.ds(0, wide), :] = jnp.zeros((wide, channels), BF16)
     field[pl.ds(wide + total, wide), :] = jnp.zeros((wide, channels), BF16)
+
+    arrived(slots, slots, 0)
+    slots_out[...] = slots[...]
+    slot_copy = pltpu.make_async_copy(slots, slots_s, lsem.at[1])
+    slot_copy.start()
+    slot_copy.wait()
+
+    def pick(d, carry):
+        fac_send[d] = table[slots_s[d, 0, 0]]
+        return carry
+
+    lax.fori_loop(0, groups, pick, 0)
+    fac_recv[me] = fac_send[me]
+    each_other(
+        lambda k: ten_copy(
+            fac_send.at[lax.rem(me + k, groups)], fac_recv.at[me], 1, k, me
+        ).start()
+    )
     act_copy.wait()
-    df_copy.wait()
-    df_send.wait_recv()
     moves[0].wait_recv()
 
-    def conv(first_cell, count, low, first):
-        part[:, pl.ds(0, count), :] = jnp.zeros((3, count, part.shape[2]), F32)
+    def products(first_cell, count, columns, first):
+        part[:, pl.ds(0, count), columns] = jnp.zeros((3, count, columns.size), F32)
 
         def tap(t, carry):
             if first:
                 tap_copy(t).wait()
             shifted = field[rows(first_cell + wide * (t // 3), count), :]
-            part[t % 3, pl.ds(0, count), :] += lax.dot_general(
-                shifted, kbuf[t], NT, preferred_element_type=F32
+            part[t % 3, pl.ds(0, count), columns] += lax.dot_general(
+                shifted, kbuf[t, columns, :], NT, preferred_element_type=F32
             )
             return carry
 
         lax.fori_loop(0, 9, tap, 0)
 
+    def joined(count, low):
         def join(r, carry):
             span = rows(r * wide, wide)
             col = lax.broadcasted_iota(jnp.int32, (wide, part.shape[2]), 0)
@@ -218,19 +267,37 @@
             + jnp.dot(low[pl.ds(0, count), :], up[y], preferred_element_type=F32)
         ).astype(BF16)
 
-    conv(cells * y, cells, lown, True)
+    products(cells * y, cells, pl.ds(0, width), True)
+
+    arrived(fac_send, fac_recv, 1)
+    for first in range(0, groups, 8):
+        span = pl.ds(first * block_cols, 8 * block_cols)
+        fac[:, span] = jnp.concatenate(
+            [fac_recv[d].astype(F32) for d in range(first, first + 8)], axis=1
+        ).astype(BF16)
+    for t in range(9):
+        kbuf[t, ranks, :] = fac[pl.ds(t * half, half), :]
+    for h in range(2):
+        up[h] = fac[pl.ds(9 * half, rank), pl.ds(h * width, width)]
+    df_send = send(kbuf.at[:, ranks], kbuf.at[:, ranks], 0)
+    df_send.start()
+    df_send.wait_recv()
+    products(cells * y, cells, pl.ds(width, rank), False)
+    joined(cells, lown)
     block[y] = finish(cells, lown)
 
     moves[1].wait_recv()
     near = chunk * y
-    conv(cells * other + near, chunk, lowp, False)
+    products(cells * other + near, chunk, pl.ds(0, width + rank), False)
+    joined(chunk, lowp)
     ysend[rows(near, chunk), :] = finish(chunk, lowp)
     near_send = send(ysend.at[rows(near, chunk)], block.at[y, rows(near, chunk)], 4)
     near_send.start()
 
     moves[2].wait_recv()
     rest = chunk * other
-    conv(cells * other + rest, chunk, lowp, False)
+    products(cells * other + rest, chunk, pl.ds(0, width + rank), False)
+    joined(chunk, lowp)
     ysend[rows(rest, chunk), :] = finish(chunk, lowp)
     rest_send = send(ysend.at[rows(rest, chunk)], block.at[y, rows(rest, chunk)], 5)
     rest_send.start()
@@ -287,12 +354,33 @@
         moved = pltpu.roll(grads, offset, 1) if offset else grads
         inside = (row >= da) & (row < high + da) & (col >= db) & (col < wide + db)
         taps[pl.ds(t * half, half), :] = jnp.where(inside, moved, 0.0).astype(BF16)
-    down_out[...] = jnp.dot(
+    each_other(
+        lambda k: ten_copy(
+            fac_send.at[lax.rem(me + k, groups)], fac_recv.at[me], 1, k, me
+        ).wait_send()
+    )
+    fin[pl.ds(0, 9 * half), :] = jnp.dot(
         taps[...], field[pl.ds(wide, total), :], preferred_element_type=F32
-    ).astype(BF16)
+    )
     up_send.wait_recv()
     for h in range(2):
-        up_out[:, pl.ds(h * width, width)] = (upp[h] + upr[h]).astype(BF16)
+        fin[pl.ds(9 * half, rank), pl.ds(h * width, width)] = upp[h] + upr[h]
+    for d in range(groups):
+        fac_send[d] = fin[:, pl.ds(d * block_cols, block_cols)].astype(BF16)
+    each_other(
+        lambda k: ten_copy(
+            fac_send.at[lax.rem(me + k, groups)], fin_recv.at[me], 2, k, me
+        ).start()
+    )
+    fin_recv[me] = fac_send[me]
+    arrived(fac_send, fin_recv, 2)
+    pieces_out[...] = fin_recv[...]
+    each_other(lambda k: ten_copy(slot_mine.at[0], slots.at[me], 0, k, me).wait_send())
+    each_other(
+        lambda k: ten_copy(
+            fac_send.at[lax.rem(me + k, groups)], fin_recv.at[me], 2, k, me
+        ).wait_send()
+    )
     for copy in [df_send, *moves, near_send, rest_send, lg_send, up_send]:
         copy.wait_send()
     for copy in outs:
@@ -309,30 +397,32 @@
     tenants, _, _, half, block_cols = down_table.shape
     rank = up_table.shape[1]
     kernel_taps = jnp.transpose(base_kernel, (0, 2, 1, 3)).reshape(9, width, channels)
-    all_tenants = lax.all_gather(sample_tenant, "ten", axis=0, tiled=True)
-    all_slots = tenant_slot[all_tenants]
-    groups = all_slots.shape[0]
-    picks = (all_slots[:, None] == jnp.arange(tenants, dtype=jnp.int32)[None, :]).astype(BF16)
+    groups = lax.axis_size("ten")
+    terms = 9 * half + rank
     table = jnp.concatenate([down_table.reshape(tenants, 9 * half, block_cols), up_table], axis=1)
-    sent = jnp.einsum("dl,lkc->dkc", picks, table, preferred_element_type=F32).astype(BF16)
-    factors = lax.all_to_all(sent, "ten", split_axis=0, concat_axis=0, tiled=True)
-    factors = jnp.transpose(factors, (1, 0, 2)).reshape(9 * half + rank, channels)
-    df = factors[: 9 * half].reshape(9, half, channels)
-    up = jnp.transpose(factors[9 * half :].reshape(rank, 2, width), (1, 0, 2))
     weight = 1.0 / (1.0 + timesteps.astype(F32) / 250.0)
 
     anywhere = pl.BlockSpec(memory_space=pl.ANY)
     vmem = pl.BlockSpec(memory_space=pltpu.VMEM)
-    block_out, down_term, up_term = pl.pallas_call(
+    block_out, pieces, slots = pl.pallas_call(
         functools.partial(core_kernel, wide=wide, chunk=chunk),
         out_shape=(
             jax.ShapeDtypeStruct((cells, channels), BF16),
-            jax.ShapeDtypeStruct((9 * half, channels), BF16),
-            jax.ShapeDtypeStruct((rank, channels), BF16),
+            jax.ShapeDtypeStruct((groups, terms, block_cols), BF16),
+            jax.ShapeDtypeStruct((groups, 1, 128), jnp.int32),
         ),
-        in_specs=[anywhere] * 4 + [vmem, pl.BlockSpec(memory_space=pltpu.SMEM)],
+        in_specs=[anywhere] * 3 + [vmem] + [pl.BlockSpec(memory_space=pltpu.SMEM)] * 3,
         out_specs=(anywhere, vmem, vmem),
         scratch_shapes=[
+            pltpu.VMEM((1, 1, 128), jnp.int32),
+            pltpu.VMEM((groups, 1, 128), jnp.int32),
+            pltpu.SMEM((groups, 1, 128), jnp.int32),
+            pltpu.VMEM((groups, terms, block_cols), BF16),
+            pltpu.VMEM((groups, terms, block_cols), BF16),
+            pltpu.VMEM((terms, channels), BF16),
+            pltpu.VMEM((terms, channels), F32),
+            pltpu.VMEM((groups, terms, block_cols), BF16),
+            pltpu.VMEM((2, rank, width), BF16),
             pltpu.VMEM((2 * cells + 2 * wide, channels), BF16),
             pltpu.VMEM((9, width + rank, channels), BF16),
             pltpu.VMEM((3, cells, width + rank), F32),
@@ -352,6 +442,8 @@
             pltpu.SemaphoreType.DMA((6,)),
             pltpu.SemaphoreType.DMA((8,)),
             pltpu.SemaphoreType.DMA((8,)),
+            pltpu.SemaphoreType.DMA((3, groups)),
+            pltpu.SemaphoreType.DMA((3, groups)),
         ],
         compiler_params=pltpu.CompilerParams(
             collective_id=0, has_side_effects=True, vmem_limit_bytes=56 * 1024 * 1024
@@ -360,13 +452,12 @@
         activations.reshape(cells, channels),
         cotangent.reshape(cells, channels),
         kernel_taps,
-        df,
-        up,
+        table,
+        sample_tenant,
+        tenant_slot,
         weight,
     )
-    terms = jnp.concatenate([down_term, up_term], axis=0).reshape(-1, groups, block_cols)
-    terms = jnp.transpose(terms, (1, 0, 2))
-    pieces = lax.all_to_all(terms, "ten", split_axis=0, concat_axis=0, tiled=True)
+    picks = (slots[:, 0, :1] == jnp.arange(tenants, dtype=jnp.int32)[None, :]).astype(BF16)
     sums = jnp.einsum("dl,dkc->lkc", picks, pieces, preferred_element_type=F32).astype(BF16)
     return (
         block_out.reshape(activations.shape),

time: 137 us -> 106 us (0.77); the launches traced: 135 us -> 106 us
  Pallas kernels: 59 us -> 95.5 us
  waiting for transfers between devices: 32.2 us -> 0 us
  starting transfers between devices: 16.4 us -> 0 us
  local copies, waits for them, and re-layouts: 15.8 us -> 6 us
  blocking collectives: 7.86 us -> 0 us
    pallas_call x1, Pallas kernels: 59 us -> 95.5 us  [local_pair(): pl.pallas_call(functools.partial(core_kernel, wide=wide, chunk=chunk), ou...]
    all_to_all x2 -> x0, waiting for transfers between devices: 32.2 us -> none  [the longest x1 16.4 us: local_pair(): lax.all_to_all(terms, 'ten', split_axis=0, concat_axis=0, tiled=True)]
    all_to_all x2 -> x0, starting transfers between devices: 16.4 us -> none  [the longest x1 8.54 us: local_pair(): lax.all_to_all(sent, 'ten', split_axis=0, concat_axis=0, tiled=True)]
    unnamed x1 -> x0, blocking collectives: 7.86 us -> none
    reshape x4 -> x0, local copies, waits for them, and re-layouts: 5.12 us -> none  [the longest x1 1.93 us: local_pair(): down_table.reshape(tenants, 9 * half, block_cols)]
    unnamed x10 -> x6, local copies, waits for them, and re-layouts: 5.22 us -> 2.02 us
    pallas_call x0 -> x1, local copies, waits for them, and re-layouts: none -> 1.97 us  [local_pair(): pl.pallas_call(functools.partial(core_kernel, wide=wide, chunk=chunk), ou...]
    transpose x1 -> x0, local copies, waits for them, and re-layouts: 1.47 us -> none  [local_pair(): terms = jnp.transpose(terms, (1, 0, 2))]
  transfers between devices with their start and end apart: 2 -> 0, of which waited for: 2 -> 0; matrix products, arithmetic and copies ran while one was open for 0% -> 0% of each run, Pallas kernels for 0% -> 0%
where the time goes in v3:
time: 106 us
  Pallas kernels  95.5 us (90%)
  local copies, waits for them, and re-layouts  6 us (6%)
  other arithmetic  2.14 us (2%)
  between operations  2.02 us (2%)
    pallas_call x1, Pallas kernels, local_pair(): pl.pallas_call(functools.partial(core_kernel, wide=wide, chunk=chunk), ou...  95.5 us
    concatenate x1, other arithmetic, local_pair(): jnp.concatenate([down_table.reshape(tenants, 9 * half, block_cols), up_ta...  2.14 us

profile of v3, /device:TPU:11, one launch (start us, length us, event | category | flops | bytes accessed | tf_op | source)
XLA Modules:
  0.0 106.0 jit_solution(1640564945475829088)
XLA Ops:
  0.6 2.1 %pad_maximum_fusion.table = bf16[16,176,80]{2,1,0:T(8,128)(2,1)} fusion(bf16[16,32,80]{2,1,0:T(8,128)(2,1)} %param.12, bf16[16,144,80]{2,1,0:T(8,128)(2,1)} %bitcast.18), kind=kLoop, calls=%fused_computation.1 | loop fusion | flops 901120 | bytes 901120 | tf_op jit(solution)/shard_map/concatenate | solution.py:402
  4.1 95.5 %shard_map.103 = (bf16[512,1280]{1,0:T(8,128)(2,1)}, bf16[16,176,80]{2,1,0:T(8,128)(2,1)}, s32[16,1,128]{2,1,0:T(1,128)}) custom-call(bf16[512,1280]{1,0:T(8,128)(2,1)} %bitcast.16, bf16[512,1280]{1,0:T(8,128)(2,1)} %bitcast.17, bf16[9,640,1280]{2,1,0:T(8,128)(2,1)} %bitcast.13, bf16[16,176,80]{2,1,0:T(8,128)(2,1)} %pad_maximum_fusion.table, ...), custom_call_target="tpu_custom_call" | custom-call | tf_op jit(solution)/shard_map/pallas_call | solution.py:407
  99.7 0.0 copy-start.1
  99.7 2.0 %copy.14 = bf16[16,176,80]{1,0,2:T(8,128)(2,1)S(1)} copy(bf16[16,176,80]{2,1,0:T(8,128)(2,1)} %get-tuple-element.8) | data formatting | bytes 901120 | tf_op jit(solution)/shard_map/pallas_call | solution.py:407
  101.6 0.0 copy-done.1
  101.7 0.4 slice_reduce_fusion
  102.0 0.3 convolution_convert_fusion
  102.4 0.0 copy-start
  102.4 1.5 %copy.15 = bf16[16,144,80]{2,1,0:T(8,128)(2,1)} copy(bf16[16,144,80]{1,0,2:T(8,128)(2,1)S(1)} %bitcast.14) | data formatting | bytes 737280 | tf_op jit(solution)/shard_map/slice | solution.py:464
  103.8 0.2 slice.13
  104.0 1.0 copy.16
  105.0 0.0 copy-done
  105.0 1.1 copy.20
Async XLA Ops:
  99.7 2.0 %copy-start.1 = (s32[16,1,128]{2,1,0:T(1,128)S(1)}, s32[16,1,128]{2,1,0:T(1,128)}, u32[]{:S(2)}) copy-start(s32[16,1,128]{2,1,0:T(1,128)} %get-tuple-element.7) | copy-start | bytes 24580
  102.4 2.6 %copy-start = (bf16[512,1280]{1,0:T(8,128)(2,1)S(1)}, bf16[512,1280]{1,0:T(8,128)(2,1)}, u32[]{:S(2)}) copy-start(bf16[512,1280]{1,0:T(8,128)(2,1)} %get-tuple-element.6) | copy-start | bytes 3932164

commit v4 on v3

--- a/solution.py
+++ b/solution.py
@@ -232,28 +232,29 @@
     act_copy.wait()
     moves[0].wait_recv()
 
-    def products(first_cell, count, columns, first):
-        part[:, pl.ds(0, count), columns] = jnp.zeros((3, count, columns.size), F32)
+    def products(first_cell, at, count, columns, first):
+        part[:, pl.ds(at, count), columns] = jnp.zeros((3, count, columns.size), F32)
 
         def tap(t, carry):
             if first:
                 tap_copy(t).wait()
             shifted = field[rows(first_cell + wide * (t // 3), count), :]
-            part[t % 3, pl.ds(0, count), columns] += lax.dot_general(
+            part[t % 3, pl.ds(at, count), columns] += lax.dot_general(
                 shifted, kbuf[t, columns, :], NT, preferred_element_type=F32
             )
             return carry
 
         lax.fori_loop(0, 9, tap, 0)
 
-    def joined(count, low):
+    def joined(at, count, low):
         def join(r, carry):
             span = rows(r * wide, wide)
             col = lax.broadcasted_iota(jnp.int32, (wide, part.shape[2]), 0)
+            held = rows(at + r * wide, wide)
             whole = (
-                part[1, span, :]
-                + jnp.where(col > 0, pltpu.roll(part[0, span, :], 1, 0), 0.0)
-                + jnp.where(col < wide - 1, pltpu.roll(part[2, span, :], wide - 1, 0), 0.0)
+                part[1, held, :]
+                + jnp.where(col > 0, pltpu.roll(part[0, held, :], 1, 0), 0.0)
+                + jnp.where(col < wide - 1, pltpu.roll(part[2, held, :], wide - 1, 0), 0.0)
             )
             bbuf[span, :] = whole[:, :width].astype(BF16)
             low[span, :] = whole[:, width:].astype(BF16)
@@ -267,7 +268,8 @@
             + jnp.dot(low[pl.ds(0, count), :], up[y], preferred_element_type=F32)
         ).astype(BF16)
 
-    products(cells * y, cells, pl.ds(0, width), True)
+    base, lows = pl.ds(0, width), pl.ds(width, rank)
+    products(cells * y, 0, cells, base, True)
 
     arrived(fac_send, fac_recv, 1)
     for first in range(0, groups, 8):
@@ -281,26 +283,28 @@
         up[h] = fac[pl.ds(9 * half, rank), pl.ds(h * width, width)]
     df_send = send(kbuf.at[:, ranks], kbuf.at[:, ranks], 0)
     df_send.start()
+    near, rest = chunk * y, chunk * other
+    moves[1].wait_recv()
+    products(cells * other + near, cells, chunk, base, False)
+    moves[2].wait_recv()
+    products(cells * other + rest, cells + chunk, chunk, base, False)
     df_send.wait_recv()
-    products(cells * y, cells, pl.ds(width, rank), False)
-    joined(cells, lown)
-    block[y] = finish(cells, lown)
-
-    moves[1].wait_recv()
-    near = chunk * y
-    products(cells * other + near, chunk, pl.ds(0, width + rank), False)
-    joined(chunk, lowp)
+
+    products(cells * other + near, cells, chunk, lows, False)
+    joined(cells, chunk, lowp)
     ysend[rows(near, chunk), :] = finish(chunk, lowp)
     near_send = send(ysend.at[rows(near, chunk)], block.at[y, rows(near, chunk)], 4)
     near_send.start()
 
-    moves[2].wait_recv()
-    rest = chunk * other
-    products(cells * other + rest, chunk, pl.ds(0, width + rank), False)
-    joined(chunk, lowp)
+    products(cells * other + rest, cells + chunk, chunk, lows, False)
+    joined(cells + chunk, chunk, lowp)
     ysend[rows(rest, chunk), :] = finish(chunk, lowp)
     rest_send = send(ysend.at[rows(rest, chunk)], block.at[y, rows(rest, chunk)], 5)
     rest_send.start()
+
+    products(cells * y, 0, cells, lows, False)
+    joined(0, cells, lown)
+    block[y] = finish(cells, lown)
 
     for copy in cot_copies:
         copy.wait()
@@ -425,7 +429,7 @@
             pltpu.VMEM((2, rank, width), BF16),
             pltpu.VMEM((2 * cells + 2 * wide, channels), BF16),
             pltpu.VMEM((9, width + rank, channels), BF16),
-            pltpu.VMEM((3, cells, width + rank), F32),
+            pltpu.VMEM((3, 2 * cells, width + rank), F32),
             pltpu.VMEM((cells, rank), BF16),
             pltpu.VMEM((chunk, rank), BF16),
             pltpu.VMEM((cells, width), BF16),

time: 106 us -> 97.3 us (0.918)
  Pallas kernels: 95.5 us -> 86.7 us
    pallas_call x1, Pallas kernels: 95.5 us -> 86.7 us  [local_pair(): pl.pallas_call(functools.partial(core_kernel, wide=wide, chunk=chunk), ou...]
where the time goes in v4:
time: 97.3 us; the launch traced here: 97.1 us
  Pallas kernels  86.7 us (89%)
  local copies, waits for them, and re-layouts  6 us (6%)
  other arithmetic  2.14 us (2%)
  between operations  2.02 us (2%)
    pallas_call x1, Pallas kernels, local_pair(): pl.pallas_call(functools.partial(core_kernel, wide=wide, chunk=chunk), ou...  86.7 us
    concatenate x1, other arithmetic, local_pair(): jnp.concatenate([down_table.reshape(tenants, 9 * half, block_cols), up_ta...  2.14 us
    unnamed x6, local copies, waits for them, and re-layouts  2.02 us
    pallas_call x1, local copies, waits for them, and re-layouts, local_pair(): pl.pallas_call(functools.partial(core_kernel, wide=wide, chunk=chunk), ou...  1.97 us

profile of v4, /device:TPU:11, one launch (start us, length us, event | category | flops | bytes accessed | tf_op | source)
XLA Modules:
  0.0 97.1 jit_solution(7187544731168295115)
XLA Ops:
  0.6 2.1 %pad_maximum_fusion.table = bf16[16,176,80]{2,1,0:T(8,128)(2,1)} fusion(bf16[16,32,80]{2,1,0:T(8,128)(2,1)} %param.12, bf16[16,144,80]{2,1,0:T(8,128)(2,1)} %bitcast.18), kind=kLoop, calls=%fused_computation.1 | loop fusion | flops 901120 | bytes 901120 | tf_op jit(solution)/shard_map/concatenate | solution.py:406
  4.1 86.7 %shard_map.103 = (bf16[512,1280]{1,0:T(8,128)(2,1)}, bf16[16,176,80]{2,1,0:T(8,128)(2,1)}, s32[16,1,128]{2,1,0:T(1,128)}) custom-call(bf16[512,1280]{1,0:T(8,128)(2,1)} %bitcast.16, bf16[512,1280]{1,0:T(8,128)(2,1)} %bitcast.17, bf16[9,640,1280]{2,1,0:T(8,128)(2,1)} %bitcast.13, bf16[16,176,80]{2,1,0:T(8,128)(2,1)} %pad_maximum_fusion.table, ...), custom_call_target="tpu_custom_call" | custom-call | tf_op jit(solution)/shard_map/pallas_call | solution.py:411
  90.8 0.0 copy-start.1
  90.8 2.0 %copy.14 = bf16[16,176,80]{1,0,2:T(8,128)(2,1)S(1)} copy(bf16[16,176,80]{2,1,0:T(8,128)(2,1)} %get-tuple-element.8) | data formatting | bytes 901120 | tf_op jit(solution)/shard_map/pallas_call | solution.py:411
  92.8 0.0 copy-done.1
  92.8 0.4 slice_reduce_fusion
  93.2 0.3 convolution_convert_fusion
  93.5 0.0 copy-start
  93.5 1.5 %copy.15 = bf16[16,144,80]{2,1,0:T(8,128)(2,1)} copy(bf16[16,144,80]{1,0,2:T(8,128)(2,1)S(1)} %bitcast.14) | data formatting | bytes 737280 | tf_op jit(solution)/shard_map/slice | solution.py:468
  95.0 0.2 slice.13
  95.1 1.0 copy.16
  96.1 0.0 copy-done
  96.1 1.1 %copy.20 = bf16[1,16,32,1280]{3,2,1,0:T(8,128)(2,1)} copy(bf16[1,16,32,1280]{3,2,1,0:T(8,128)(2,1)S(1)} %bitcast.15) | data formatting | bytes 2621440
Async XLA Ops:
  90.8 2.0 %copy-start.1 = (s32[16,1,128]{2,1,0:T(1,128)S(1)}, s32[16,1,128]{2,1,0:T(1,128)}, u32[]{:S(2)}) copy-start(s32[16,1,128]{2,1,0:T(1,128)} %get-tuple-element.7) | copy-start | bytes 24580
  93.5 2.6 %copy-start = (bf16[512,1280]{1,0:T(8,128)(2,1)S(1)}, bf16[512,1280]{1,0:T(8,128)(2,1)}, u32[]{:S(2)}) copy-start(bf16[512,1280]{1,0:T(8,128)(2,1)} %get-tuple-element.6) | copy-start | bytes 3932164
